TPU v7x, 512 devices: a whole 4x8x8 slice. The times are simulated.
512 devices in a mesh: outer: 8 (over x, z_lo), inner: 64 (over y, z_hi, core).
Axes of the slice: x: 4, y: 8, z: 8 (z_hi: 4, z_lo: 2; z = z_hi * 2 + z_lo), core: 2. Of those that a mesh axis runs over, the one named last changes fastest.
Arguments:
- queries: bfloat16 [131072, 1024], P(('outer', 'inner')), may hold values from -160 to 160
- key_rows: bfloat16 [131072, 128], P(('outer', 'inner')), may hold values from -4 to 4
- value_rows: bfloat16 [131072, 128], P(('outer', 'inner')), may hold values from -5 to 5
- grad_out: bfloat16 [131072, 1024], P(('outer', 'inner')), may hold values from -5 to 5
- doc_starts: int32 [341], replicated, may hold values from 0 to 131071, as said below
- doc_ids: int32 [131072], P(('outer', 'inner')), may hold values from 0 to 340, as said below
Outputs:
- attended: bfloat16 [131072, 1024], P(('outer', 'inner'))
- query_grad: bfloat16 [131072, 1024], P(('outer', 'inner'))
- key_grad: bfloat16 [131072, 128], P(('outer', 'inner'))
- value_grad: bfloat16 [131072, 128], P(('outer', 'inner'))
Inputs may be any that keep to these rules, and one draw needn't show every extreme that they name: doc_starts[0] = 0 and the starts rise; each document runs up to the next start (the last to 131072); every document holds 1 to 767 tokens, and one holds exactly 767. doc_ids[t] is the document whose range holds position t.
All inputs are finite; a program needn't handle non-finite values.
Results may differ from a plain program's by a relative error of at most 0.028.
Values may be sent and summed in bfloat16 or wider, within the bound.
A program may use at most 64 MiB of HBM per device.

v0:
```python
import math

import jax
import jax.numpy as jnp
from jax import lax
from jax.sharding import PartitionSpec as P

LEVELS = 2


def from_behind(value, axis, by):
    devices = lax.axis_size(axis)
    return lax.ppermute(value, axis, [(i, (i + by) % devices) for i in range(devices)])


def shifted(value, axis, steps):
    count = lax.axis_size(axis)
    initial, last = (max(0, -steps), min(count, count - steps))
    return lax.ppermute(value, axis, [(source, source + steps) for source in range(initial, last)])


def contract_last(left, right):
    return lax.dot_general(
        left, right, (((1,), (1,)), ((), ())), preferred_element_type=jnp.float32
    )


def contract_first(left, right):
    return lax.dot_general(
        left, right, (((0,), (0,)), ((), ())), preferred_element_type=jnp.float32
    )


def local(queries, key_rows, value_rows, grad_out, doc_starts, doc_ids):
    tok_count = key_rows.shape[0]
    head_dim = key_rows.shape[1]
    head_count = queries.shape[1] // head_dim
    span_blocks = 2**LEVELS
    score_scale = 1.0 / math.sqrt(head_dim)
    inner_count = lax.axis_size("inner")
    inner_place = lax.axis_index("inner")
    my_block = lax.axis_index("outer") * inner_count + inner_place
    block_ages = jnp.arange(span_blocks, dtype=jnp.int32)
    own_older = (block_ages <= inner_place)[:, None, None]
    buffer = jnp.concatenate([key_rows, value_rows], axis=1)[None]
    for level_index in range(LEVELS):
        arrived = from_behind(buffer, "inner", 2**level_index)
        buffer = jnp.concatenate([buffer, arrived], axis=0)
    across = shifted(buffer, "outer", 1)
    buffer = jnp.where(own_older, buffer, across)
    positions = my_block * tok_count + jnp.arange(tok_count, dtype=jnp.int32)
    doc_index = jnp.arange(doc_starts.shape[0], dtype=jnp.int32)
    token_starts = jnp.sum(
        jnp.where(doc_ids[:, None] == doc_index[None, :], doc_starts[None, :], 0), axis=1
    )
    query_rows = queries.reshape(tok_count * head_count, head_dim)
    grad_rows = grad_out.reshape(tok_count * head_count, head_dim)

    def allowed_for(block_age):
        key_positions = (my_block - block_age) * tok_count + jnp.arange(tok_count, dtype=jnp.int32)
        return (key_positions[None, :] >= token_starts[:, None]) & (
            key_positions[None, :] <= positions[:, None]
        )

    def scores_for(key_block, allowed):
        scores = contract_last(query_rows, key_block) * score_scale
        return jnp.where(
            allowed[:, None, :], scores.reshape(tok_count, head_count, tok_count), -jnp.inf
        )

    def stats_step(state_pair, block_item):
        pair_block, block_age = block_item
        allowed = allowed_for(block_age)
        row_max, row_sum = state_pair
        scores = scores_for(pair_block[:, :head_dim], allowed)
        new_max = jnp.maximum(row_max, jnp.max(scores, axis=-1))
        new_sum = row_sum * jnp.exp(row_max - new_max) + jnp.sum(
            jnp.exp(scores - new_max[..., None]), axis=-1
        )
        return ((new_max, new_sum), None)

    stats_init = (
        jnp.full((tok_count, head_count), -jnp.inf, jnp.float32),
        jnp.zeros((tok_count, head_count), jnp.float32),
    )
    row_max, row_sum = lax.scan(stats_step, stats_init, (buffer, block_ages))[0]
    log_total = row_max + jnp.log(row_sum)

    def output_step(out_sum, block_item):
        pair_block, block_age = block_item
        allowed = allowed_for(block_age)
        scores = scores_for(pair_block[:, :head_dim], allowed)
        weights_low = (
            jnp.exp(scores - log_total[..., None])
            .astype(jnp.bfloat16)
            .reshape(tok_count * head_count, tok_count)
        )
        return (
            out_sum
            + jnp.dot(weights_low, pair_block[:, head_dim:], preferred_element_type=jnp.float32),
            None,
        )

    out_init = jnp.zeros((tok_count * head_count, head_dim), jnp.float32)
    out_sum = lax.scan(output_step, out_init, (buffer, block_ages))[0]
    attended = lax.optimization_barrier(out_sum.astype(jnp.bfloat16))
    delta_rows = jnp.sum(
        grad_rows.astype(jnp.float32) * attended.astype(jnp.float32), axis=-1
    ).reshape(tok_count, head_count)

    def grad_step(query_grad, block_item):
        pair_block, block_age = block_item
        allowed = allowed_for(block_age)
        key_block = pair_block[:, :head_dim]
        value_block = pair_block[:, head_dim:]
        scores = scores_for(key_block, allowed)
        weights = jnp.exp(scores - log_total[..., None])
        weights_low = weights.astype(jnp.bfloat16).reshape(tok_count * head_count, tok_count)
        grad_weights = contract_last(grad_rows, value_block).reshape(
            tok_count, head_count, tok_count
        )
        grad_scores = (weights * (grad_weights - delta_rows[..., None]) * score_scale).astype(
            jnp.bfloat16
        )
        grad_scores = grad_scores.reshape(tok_count * head_count, tok_count)
        new_grad = query_grad + jnp.dot(grad_scores, key_block, preferred_element_type=jnp.float32)
        key_part = contract_first(grad_scores, query_rows)
        value_part = contract_first(weights_low, grad_rows)
        return (new_grad, jnp.concatenate([key_part, value_part], axis=1))

    query_grad, partials = lax.scan(
        grad_step, jnp.zeros((tok_count * head_count, head_dim), jnp.float32), (buffer, block_ages)
    )
    across = shifted(partials.astype(jnp.bfloat16), "outer", -1).astype(partials.dtype)
    partials = jnp.where(own_older, partials, across)
    for level_index in reversed(range(LEVELS)):
        half_count = 2**level_index
        arrived = from_behind(partials[half_count:], "inner", -half_count)
        partials = partials[:half_count] + arrived
    key_grad = partials[0][:, :head_dim].astype(jnp.bfloat16)
    value_grad = partials[0][:, head_dim:].astype(jnp.bfloat16)
    return (
        attended.reshape(tok_count, head_count * head_dim),
        query_grad.astype(jnp.bfloat16).reshape(tok_count, head_count * head_dim),
        key_grad,
        value_grad,
    )


def solution(mesh):
    in_specs = (
        P(("outer", "inner"), None),
        P(("outer", "inner"), None),
        P(("outer", "inner"), None),
        P(("outer", "inner"), None),
        P(),
        P(("outer", "inner")),
    )
    out_specs = (
        P(("outer", "inner"), None),
        P(("outer", "inner"), None),
        P(("outer", "inner"), None),
        P(("outer", "inner"), None),
    )
    return jax.shard_map(local, mesh=mesh, in_specs=in_specs, out_specs=out_specs, check_vma=False)
```

profile of v0, /device:TPU:21, one launch (start us, length us, event | category | flops | bytes accessed | tf_op | source)
XLA Modules:
  0.0 181.9 jit_solution(16258163492330179744)
XLA Ops:
  0.7 1.0 maximum_bitcast_fusion.1
  1.6 6.4 %collective-permute-start = (bf16[1,256,256]{2,1,0:T(8,128)(2,1)S(1)}, bf16[1,256,256]{2,1,0:T(8,128)(2,1)S(1)}, u32[]{:S(2)}, u32[]{:S(2)}) collective-permute-start(bf16[1,256,256]{2,1,0:T(8,128)(2,1)S(1)} %maximum_bitcast_fusion.1), channel_id=1, source_target_pairs={{0,1},{1,2},{2,3},{3,4},{4,5},{5,6},{6,7},{7,8},{8,9},{9,10},{10,1... | collective-permute-start | bytes 393224 | tf_op jit(solution)/shard_map/ppermute | solution.py:13
  8.0 1.9 %collective-permute-done = bf16[1,256,256]{2,1,0:T(8,128)(2,1)S(1)} collective-permute-done((bf16[1,256,256]{2,1,0:T(8,128)(2,1)S(1)}, bf16[1,256,256]{2,1,0:T(8,128)(2,1)S(1)}, u32[]{:S(2)}, u32[]{:S(2)}) %collective-permute-start) | collective-permute-done | bytes 131104 | tf_op jit(solution)/shard_map/ppermute | solution.py:13
  10.0 7.0 %collective-permute-start.1 = (bf16[2,256,256]{2,1,0:T(8,128)(2,1)S(1)}, bf16[2,256,256]{2,1,0:T(8,128)(2,1)S(1)}, u32[]{:S(2)}, u32[]{:S(2)}) collective-permute-start(bf16[2,256,256]{2,1,0:T(8,128)(2,1)S(1)} %pad_maximum_fusion.1), channel_id=1, source_target_pairs={{0,2},{1,3},{2,4},{3,5},{4,6},{5,7},{6,8},{7,9},{8,10},{9,11},{10,... | collective-permute-start | bytes 786440 | tf_op jit(solution)/shard_map/ppermute | solution.py:13
  17.0 8.5 %collective-permute-done.1 = bf16[2,256,256]{2,1,0:T(8,128)(2,1)S(1)} collective-permute-done((bf16[2,256,256]{2,1,0:T(8,128)(2,1)S(1)}, bf16[2,256,256]{2,1,0:T(8,128)(2,1)S(1)}, u32[]{:S(2)}, u32[]{:S(2)}) %collective-permute-start.1) | collective-permute-done | bytes 262176 | tf_op jit(solution)/shard_map/ppermute | solution.py:13
  25.5 6.5 %collective-permute-start.2 = (bf16[4,256,256]{2,1,0:T(8,128)(2,1)S(1)}, bf16[4,256,256]{2,1,0:T(8,128)(2,1)S(1)}, u32[]{:S(2)}, u32[]{:S(2)}) collective-permute-start(bf16[4,256,256]{2,1,0:T(8,128)(2,1)S(1)} %pad_maximum_fusion), channel_id=1, source_target_pairs={{0,64},{64,128},{128,192},{192,256},{256,320},{320,384},{384,448},... | collective-permute-start | bytes 1572872 | tf_op jit(solution)/shard_map/ppermute | solution.py:19
  32.8 8.8 %collective-permute-done.2 = bf16[4,256,256]{2,1,0:T(8,128)(2,1)S(1)} collective-permute-done((bf16[4,256,256]{2,1,0:T(8,128)(2,1)S(1)}, bf16[4,256,256]{2,1,0:T(8,128)(2,1)S(1)}, u32[]{:S(2)}, u32[]{:S(2)}) %collective-permute-start.2) | collective-permute-done | bytes 524320 | tf_op jit(solution)/shard_map/ppermute | solution.py:19
  41.6 0.9 broadcast_select_fusion
  42.5 23.2 %while.39 = (s32[]{:T(128)}, f32[256,8]{1,0:T(8,128)S(1)}, f32[256,8]{1,0:T(8,128)}, s32[4]{0:T(128)S(1)}, s32[]{:T(128)}, /*index=5*/s32[256]{0:T(256)S(1)}, bf...) while((s32[]{:T(128)}, f32[256,8]{1,0:T(8,128)S(1)}, ...), condition=%wide.region_4.5_spmd.clone, body=%wide.region_1.4_spmd.clone.sunk | while | flops 137046528 | bytes 7435448 | solution.py:86
  43.9 0.9 dynamic-slice_bitcast_fusion.8
  49.0 0.9 dynamic-slice_bitcast_fusion.8
  52.0 1.6 fusion.88
  55.0 0.9 dynamic-slice_bitcast_fusion.8
  58.0 1.6 fusion.88
  61.1 0.9 dynamic-slice_bitcast_fusion.8
  64.0 1.6 fusion.88
  65.7 0.9 log_add_fusion
  67.2 24.4 %while.40 = (s32[]{:T(128)}, f32[2048,128]{1,0:T(8,128)}, s32[4]{0:T(128)S(1)}, s32[]{:T(128)}, s32[256]{0:T(256)S(1)}, /*index=5*/bf16[4,256,256]{2,1,0:T(8,128...) while((s32[]{:T(128)}, f32[2048,128]{1,0:T(8,128)}, ...), condition=%wide.wide.region_6.7_spmd.clone, body=%wide.wide.region_5.6_spmd.clone.sunk | while | flops 271254016 | bytes 5256383 | solution.py:105
  68.6 0.9 dynamic-slice_bitcast_fusion.9
  70.4 2.0 %convolution_add_fusion.6 = f32[2048,128]{1,0:T(8,128)} fusion(pred[2048,256]{0,1:T(32,128)(4,1)S(1)} %copy.36, bf16[2048,128]{1,0:T(8,128)(2,1)S(1)} %get-tuple-element.712, f32[2048,128]{1,0:T(8,128)} %get-tuple-element.694, f32[2048]{0:T(1024)S(1)} %get-tuple-element.715, pred[]{:T(512)S(6)} %compare.12, ...), kind=kOutput, calls=%fused_computation.22.clone.clone.1 | convolution fusion | flops 271056896 | bytes 3284993 | tf_op jit(solution)/shard_map/while/body/eval_jaxpr/dot_general | solution.py:100
  73.8 0.9 dynamic-slice_bitcast_fusion.9
  75.6 3.2 %convolution_add_fusion.6 = f32[2048,128]{1,0:T(8,128)} fusion(pred[2048,256]{0,1:T(32,128)(4,1)S(1)} %copy.36, bf16[2048,128]{1,0:T(8,128)(2,1)S(1)} %get-tuple-element.712, f32[2048,128]{1,0:T(8,128)} %get-tuple-element.694, f32[2048]{0:T(1024)S(1)} %get-tuple-element.715, pred[]{:T(512)S(6)} %compare.12, ...), kind=kOutput, calls=%fused_computation.22.clone.clone.1 | convolution fusion | flops 271056896 | bytes 3284993 | tf_op jit(solution)/shard_map/while/body/eval_jaxpr/dot_general | solution.py:100
  80.2 0.9 dynamic-slice_bitcast_fusion.9
  82.0 3.2 %convolution_add_fusion.6 = f32[2048,128]{1,0:T(8,128)} fusion(pred[2048,256]{0,1:T(32,128)(4,1)S(1)} %copy.36, bf16[2048,128]{1,0:T(8,128)(2,1)S(1)} %get-tuple-element.712, f32[2048,128]{1,0:T(8,128)} %get-tuple-element.694, f32[2048]{0:T(1024)S(1)} %get-tuple-element.715, pred[]{:T(512)S(6)} %compare.12, ...), kind=kOutput, calls=%fused_computation.22.clone.clone.1 | convolution fusion | flops 271056896 | bytes 3284993 | tf_op jit(solution)/shard_map/while/body/eval_jaxpr/dot_general | solution.py:100
  86.6 0.9 dynamic-slice_bitcast_fusion.9
  88.4 3.2 %convolution_add_fusion.6 = f32[2048,128]{1,0:T(8,128)} fusion(pred[2048,256]{0,1:T(32,128)(4,1)S(1)} %copy.36, bf16[2048,128]{1,0:T(8,128)(2,1)S(1)} %get-tuple-element.712, f32[2048,128]{1,0:T(8,128)} %get-tuple-element.694, f32[2048]{0:T(1024)S(1)} %get-tuple-element.715, pred[]{:T(512)S(6)} %compare.12, ...), kind=kOutput, calls=%fused_computation.22.clone.clone.1 | convolution fusion | flops 271056896 | bytes 3284993 | tf_op jit(solution)/shard_map/while/body/eval_jaxpr/dot_general | solution.py:100
  91.6 1.4 convert_element_type.32
  93.8 28.4 %while.41 = (s32[]{:T(128)}, f32[2048,128]{1,0:T(8,128)S(1)}, f32[4,256,256]{2,1,0:T(8,128)}, s32[4]{0:T(128)S(1)}, s32[]{:T(128)}, /*index=5*/s32[256]{0:T(256)...) while((s32[]{:T(128)}, f32[2048,128]{1,0:T(8,128)S(1)}, ...), condition=%wide.wide.region_9.10_spmd.clone, body=%wide.wide.region_8.9_spmd.clone.sunk | while | flops 676069888 | bytes 18175196 | solution.py:131
  95.2 0.9 dynamic-slice_bitcast_fusion.10
  99.1 0.9 convolution_add_fusion.7
  100.2 0.7 constant_dynamic-update-slice_fusion.3
  102.3 0.9 dynamic-slice_bitcast_fusion.10
  106.2 0.9 convolution_add_fusion.7
  109.4 0.9 dynamic-slice_bitcast_fusion.10
  113.3 0.9 convolution_add_fusion.7
  114.3 0.7 constant_dynamic-update-slice_fusion.3
  116.4 0.9 dynamic-slice_bitcast_fusion.10
  120.4 0.9 convolution_add_fusion.7
  121.4 0.7 constant_dynamic-update-slice_fusion.3
  122.1 1.4 convert_element_type.36
  123.5 4.1 %collective-permute-start.3 = (bf16[4,256,256]{2,1,0:T(8,128)(2,1)S(1)}, bf16[4,256,256]{2,1,0:T(8,128)(2,1)S(1)}, u32[]{:S(2)}, u32[]{:S(2)}) collective-permute-start(bf16[4,256,256]{2,1,0:T(8,128)(2,1)S(1)} %convert_element_type.36), channel_id=1, source_target_pairs={{64,0},{128,64},{192,128},{256,192},{320,256},{384,320},{448,384},... | collective-permute-start | bytes 1572872 | tf_op jit(solution)/shard_map/ppermute | solution.py:19
  127.6 9.4 %collective-permute-done.3 = bf16[4,256,256]{2,1,0:T(8,128)(2,1)S(1)} collective-permute-done((bf16[4,256,256]{2,1,0:T(8,128)(2,1)S(1)}, bf16[4,256,256]{2,1,0:T(8,128)(2,1)S(1)}, u32[]{:S(2)}, u32[]{:S(2)}) %collective-permute-start.3) | collective-permute-done | bytes 524320 | tf_op jit(solution)/shard_map/ppermute | solution.py:19
  137.2 2.1 %collective-permute-start.4 = (f32[2,256,256]{2,1,0:T(8,128)S(1)}, f32[2,256,256]{2,1,0:T(8,128)S(1)}, u32[]{:S(2)}, u32[]{:S(2)}) collective-permute-start(f32[2,256,256]{2,1,0:T(8,128)S(1)} %slice.52), channel_id=1, source_target_pairs={{0,62},{1,63},{2,0},{3,1},{4,2},{5,3},{6,4},{7,5},{8,6},{9,7},{10,... | collective-permute-start | bytes 1572872 | tf_op jit(solution)/shard_map/ppermute | solution.py:13
  139.3 26.2 %collective-permute-done.4 = f32[2,256,256]{2,1,0:T(8,128)S(1)} collective-permute-done((f32[2,256,256]{2,1,0:T(8,128)S(1)}, f32[2,256,256]{2,1,0:T(8,128)S(1)}, u32[]{:S(2)}, u32[]{:S(2)}) %collective-permute-start.4) | collective-permute-done | bytes 524320 | tf_op jit(solution)/shard_map/ppermute | solution.py:13
  165.6 6.3 %collective-permute-start.5 = (f32[1,256,256]{2,1,0:T(8,128)S(1)}, f32[1,256,256]{2,1,0:T(8,128)S(1)}, u32[]{:S(2)}, u32[]{:S(2)}) collective-permute-start(f32[1,256,256]{2,1,0:T(8,128)S(1)} %slice.54), channel_id=1, source_target_pairs={{0,63},{1,0},{2,1},{3,2},{4,3},{5,4},{6,5},{7,6},{8,7},{9,8},{10,9... | collective-permute-start | bytes 786440 | tf_op jit(solution)/shard_map/ppermute | solution.py:13
  171.9 1.0 reshape.207
  172.9 1.0 reshape.209
  174.0 7.3 %collective-permute-done.5 = f32[1,256,256]{2,1,0:T(8,128)S(1)} collective-permute-done((f32[1,256,256]{2,1,0:T(8,128)S(1)}, f32[1,256,256]{2,1,0:T(8,128)S(1)}, u32[]{:S(2)}, u32[]{:S(2)}) %collective-permute-start.5) | collective-permute-done | bytes 262176 | tf_op jit(solution)/shard_map/ppermute | solution.py:13
  (156 shorter events, 37.2 us)
Async XLA Ops:
  0.6 31.5 %copy-start.5 = (bf16[256,1024]{1,0:T(8,128)(2,1)S(1)}, bf16[256,1024]{1,0:T(8,128)(2,1)}, u32[]{:S(2)}) copy-start(bf16[256,1024]{1,0:T(8,128)(2,1)} %param.12) | copy-start | bytes 1572868
  0.6 31.7 %copy-start.6 = (bf16[256,1024]{1,0:T(8,128)(2,1)S(1)}, bf16[256,1024]{1,0:T(8,128)(2,1)}, u32[]{:S(2)}) copy-start(bf16[256,1024]{1,0:T(8,128)(2,1)} %param.15) | copy-start | bytes 1572868
  0.7 32.0 %copy-start.8 = (s32[256]{0:T(256)S(1)}, s32[256]{0:T(256)}, u32[]{:S(2)}) copy-start(s32[256]{0:T(256)} %param.17) | copy-start | bytes 3076
  0.7 32.0 %copy-start.7 = (s32[341]{0:T(512)S(1)}, s32[341]{0:T(512)}, u32[]{:S(2)}) copy-start(s32[341]{0:T(512)} %param.16) | copy-start | bytes 4096
  1.6 8.3 %collective-permute-start = (bf16[1,256,256]{2,1,0:T(8,128)(2,1)S(1)}, bf16[1,256,256]{2,1,0:T(8,128)(2,1)S(1)}, u32[]{:S(2)}, u32[]{:S(2)}) collective-permute-start(bf16[1,256,256]{2,1,0:T(8,128)(2,1)S(1)} %maximum_bitcast_fusion.1), channel_id=1, source_target_pairs={{0,1},{1,2},{2,3},{3,4},{4,5},{5,6},{6,7},{7,8},{8,9},{9,10},{10,1... | collective-permute-start | bytes 393224 | tf_op jit(solution)/shard_map/ppermute | solution.py:13
  10.0 15.5 %collective-permute-start.1 = (bf16[2,256,256]{2,1,0:T(8,128)(2,1)S(1)}, bf16[2,256,256]{2,1,0:T(8,128)(2,1)S(1)}, u32[]{:S(2)}, u32[]{:S(2)}) collective-permute-start(bf16[2,256,256]{2,1,0:T(8,128)(2,1)S(1)} %pad_maximum_fusion.1), channel_id=1, source_target_pairs={{0,2},{1,3},{2,4},{3,5},{4,6},{5,7},{6,8},{7,9},{8,10},{9,11},{10,... | collective-permute-start | bytes 786440 | tf_op jit(solution)/shard_map/ppermute | solution.py:13
  25.5 16.0 %collective-permute-start.2 = (bf16[4,256,256]{2,1,0:T(8,128)(2,1)S(1)}, bf16[4,256,256]{2,1,0:T(8,128)(2,1)S(1)}, u32[]{:S(2)}, u32[]{:S(2)}) collective-permute-start(bf16[4,256,256]{2,1,0:T(8,128)(2,1)S(1)} %pad_maximum_fusion), channel_id=1, source_target_pairs={{0,64},{64,128},{128,192},{192,256},{256,320},{320,384},{384,448},... | collective-permute-start | bytes 1572872 | tf_op jit(solution)/shard_map/ppermute | solution.py:19
  66.6 0.6 copy-start.4
  91.6 1.7 copy-start
  93.0 0.8 copy-start.1
  122.1 14.8 %copy-start.3 = (f32[4,256,256]{2,1,0:T(8,128)S(1)}, f32[4,256,256]{2,1,0:T(8,128)}, u32[]{:S(2)}) copy-start(f32[4,256,256]{2,1,0:T(8,128)} %get-tuple-element.166) | copy-start | bytes 3145732
  123.5 13.4 %collective-permute-start.3 = (bf16[4,256,256]{2,1,0:T(8,128)(2,1)S(1)}, bf16[4,256,256]{2,1,0:T(8,128)(2,1)S(1)}, u32[]{:S(2)}, u32[]{:S(2)}) collective-permute-start(bf16[4,256,256]{2,1,0:T(8,128)(2,1)S(1)} %convert_element_type.36), channel_id=1, source_target_pairs={{64,0},{128,64},{192,128},{256,192},{320,256},{384,320},{448,384},... | collective-permute-start | bytes 1572872 | tf_op jit(solution)/shard_map/ppermute | solution.py:19
  137.1 34.7 %copy-start.2 = (bf16[2048,128]{1,0:T(8,128)(2,1)S(1)}, bf16[2048,128]{1,0:T(8,128)(2,1)}, u32[]{:S(2)}) copy-start(bf16[2048,128]{1,0:T(8,128)(2,1)} %copy-done.1) | copy-start | bytes 1572868
  137.2 28.3 %collective-permute-start.4 = (f32[2,256,256]{2,1,0:T(8,128)S(1)}, f32[2,256,256]{2,1,0:T(8,128)S(1)}, u32[]{:S(2)}, u32[]{:S(2)}) collective-permute-start(f32[2,256,256]{2,1,0:T(8,128)S(1)} %slice.52), channel_id=1, source_target_pairs={{0,62},{1,63},{2,0},{3,1},{4,2},{5,3},{6,4},{7,5},{8,6},{9,7},{10,... | collective-permute-start | bytes 1572872 | tf_op jit(solution)/shard_map/ppermute | solution.py:13
  165.6 15.6 %collective-permute-start.5 = (f32[1,256,256]{2,1,0:T(8,128)S(1)}, f32[1,256,256]{2,1,0:T(8,128)S(1)}, u32[]{:S(2)}, u32[]{:S(2)}) collective-permute-start(f32[1,256,256]{2,1,0:T(8,128)S(1)} %slice.54), channel_id=1, source_target_pairs={{0,63},{1,0},{2,1},{3,2},{4,3},{5,4},{6,5},{7,6},{8,7},{9,8},{10,9... | collective-permute-start | bytes 786440 | tf_op jit(solution)/shard_map/ppermute | solution.py:13
where the time goes:
time: 183 us; the launch traced here: 182 us
  waiting for transfers between devices  62 us (34%)
  local copies, waits for them, and re-layouts  37.4 us (20%)
  starting transfers between devices  32.3 us (18%)
  matrix products  25.6 us (14%)
  other arithmetic  15 us (8%)
  loops' own time  8.61 us (5%)
    ppermute x4, waiting for transfers between devices, from_behind(): lax.ppermute(value, axis, [(i, (i + by) % devices) for i in range(devices)])  43.9 us
    ppermute x4, starting transfers between devices, from_behind(): lax.ppermute(value, axis, [(i, (i + by) % devices) for i in range(devices)])  21.7 us
    ppermute x2, waiting for transfers between devices, shifted(): lax.ppermute(value, axis, [(source, source + steps) for source in range(i...  18.1 us
    dot_general x4, matrix products, output_step(): jnp.dot(weights_low, pair_block[:, head_dim:], preferred_element_type=jnp...  11.6 us
    squeeze x12, local copies, waits for them, and re-layouts, local(): row_max, row_sum = lax.scan(stats_step, stats_init, (buffer, block_ages))[0]  11 us
    ppermute x2, starting transfers between devices, shifted(): lax.ppermute(value, axis, [(source, source + steps) for source in range(i...  10.6 us
    broadcast_in_dim x24, local copies, waits for them, and re-layouts, scores_for(): jnp.where(allowed[:, None, :], scores.reshape(tok_count, head_count, tok_...  10.3 us
    dynamic_slice x12, local copies, waits for them, and re-layouts, local(): row_max, row_sum = lax.scan(stats_step, stats_init, (buffer, block_ages))[0]  7.11 us
  transfers between devices with their start and end apart: 6, of which 6 were waited for; matrix products, arithmetic and copies ran while one was open for 1% of the time, Pallas kernels for 0%

commit v1 on v0

v1 whole, which is shorter than its diff:
```python
import functools
import math

import jax
import jax.numpy as jnp
from jax import lax
from jax.experimental import pallas as pl
from jax.experimental.pallas import tpu as pltpu
from jax.sharding import PartitionSpec as P

MESH = pl.DeviceIdType.MESH
SPAN = 4
CHUNK = 32
GROUP = 2
MASKED = -1e30
VMEM_BYTES = 48 * 2**20
F32 = jnp.float32
BF16 = jnp.bfloat16


def dot(left, right):
    return jnp.dot(left, right, preferred_element_type=F32)


def kernel(
    sizes,
    q_in, k_in, v_in, g_in, doc_in,
    att_out, dq_out, dk_out, dv_out,
    docs, q, g, qt, gt, kw, vw, kt, vt, bias, probs, dprobs, low, grad_low, row_max, row_sum, row_dot, block_max,
    relay_k, relay_v, part_k, part_v, send_k, send_v, got_k, got_v, att, dq, dk, dv,
    local_sem, out_sem, send_sem, recv_sem,
):
    outer_count, inner_count, tok, heads, dim = sizes
    total = outer_count * inner_count
    score_scale = 1.0 / math.sqrt(dim)
    to_log2 = score_scale * math.log2(math.e)
    me = lax.axis_index("outer") * inner_count + lax.axis_index("inner")
    odd = lax.rem(me, 2)

    def device(offset):
        place = lax.rem(me + offset + total, total)
        return (lax.div(place, inner_count), lax.rem(place, inner_count))

    sibling = device(1 - 2 * odd)

    has_two_before = me >= 2
    has_three_before = me >= 3
    has_two_after = me + 2 < total
    has_three_after = me + 3 < total
    is_odd = odd == 1
    is_even = odd == 0

    step = lax.div(lax.rem(me, 8), 2)
    relay = device(jnp.where(step == 0, 6, -2))
    relayed_from = device(jnp.where(step == 3, -6, 2))
    relay_target = jnp.where(step == 3, -3, 5)
    has_relay_target = me + relay_target < total
    relay_source = device(jnp.where(step == 2, 3, -5))

    for age in range(1, SPAN):

        @pl.when(me < age)
        def _(age=age):
            kw[age] = jnp.zeros_like(kw[age])
            vw[age] = jnp.zeros_like(vw[age])

    @pl.when(me + 3 >= total)
    def _():
        for slot in (0, 2):
            got_k[slot] = jnp.zeros_like(got_k[slot])
            got_v[slot] = jnp.zeros_like(got_v[slot])

    barrier = pltpu.get_barrier_semaphore()

    def greet(place):
        pl.semaphore_signal(barrier, inc=1, device_id=place, device_id_type=MESH)

    greet(sibling)

    @pl.when(has_two_before)
    def _():
        greet(device(-2))

    @pl.when(is_even & has_three_before)
    def _():
        greet(relay_source)

    @pl.when(is_odd & has_relay_target)
    def _():
        greet(relayed_from)

    key_load = pltpu.make_async_copy(k_in, kw.at[0], local_sem.at[0])
    value_load = pltpu.make_async_copy(v_in, vw.at[0], local_sem.at[1])
    doc_load = pltpu.make_async_copy(doc_in, docs, local_sem.at[2])
    head_loads = []
    for head in range(heads):
        here, there = pl.ds(head * dim, dim), pl.ds(head * tok, tok)
        head_loads += [
            pltpu.make_async_copy(q_in.at[:, here], q.at[there], local_sem.at[3 + head]),
            pltpu.make_async_copy(g_in.at[:, here], g.at[there], local_sem.at[3 + heads + head]),
        ]
    for copy in [key_load, value_load, doc_load] + head_loads:
        copy.start()

    def remote(source, target, place, number):
        return pltpu.make_async_remote_copy(
            src_ref=source,
            dst_ref=target,
            send_sem=send_sem.at[number],
            recv_sem=recv_sem.at[number],
            device_id=place,
            device_id_type=MESH,
        )

    def pair(keys, values, target_slot, place, number):
        return (
            remote(keys, kw.at[target_slot], place, number),
            remote(values, vw.at[target_slot], place, number + 1),
        )

    to_next = pair(kw.at[0], vw.at[0], 2, device(2), 0)
    own_to_sibling = pair(kw.at[0], vw.at[0], 1, sibling, 2)
    passed_to_sibling = pair(kw.at[2], vw.at[2], 1, sibling, 2)
    passed_on = pair(kw.at[2], vw.at[2], 3, sibling, 4)
    relay_in = (
        remote(kw.at[0], relay_k, relay, 12),
        remote(vw.at[0], relay_v, relay, 13),
    )
    relay_out = pair(relay_k, relay_v, 3, device(relay_target), 4)
    third = (
        remote(send_k.at[0], got_k.at[0], device(2 * odd - 3), 6),
        remote(send_v.at[0], got_v.at[0], device(2 * odd - 3), 7),
    )
    first = (
        remote(send_k.at[1], got_k.at[1], sibling, 8),
        remote(send_v.at[1], got_v.at[1], sibling, 9),
    )
    second = (
        remote(send_k.at[2], got_k.at[2], device(-2), 10),
        remote(send_v.at[2], got_v.at[2], device(-2), 11),
    )

    def start(copies):
        for copy in copies:
            copy.start()

    def received(copies):
        for copy in copies:
            copy.wait_recv()

    def sent(copies):
        for copy in copies:
            copy.wait_send()

    key_load.wait()
    value_load.wait()
    targets = 1 + jnp.where(has_two_after, 1, 0)
    targets += jnp.where(is_odd & has_three_after, 1, 0)
    targets += jnp.where(is_odd & has_relay_target, 1, 0)
    pl.semaphore_wait(barrier, targets)

    @pl.when(is_even)
    def _():
        start(own_to_sibling)

    @pl.when(is_odd & has_two_after)
    def _():
        start(to_next)

    @pl.when(is_odd & has_three_after)
    def _():
        start(relay_in)

    doc_load.wait()
    first_row = (me * tok).astype(F32)
    doc_starts = jnp.broadcast_to(docs[...][None, :].astype(F32), (tok, docs.shape[0])) - first_row
    positions = lax.broadcasted_iota(jnp.int32, doc_starts.shape, 0).astype(F32)
    starts = jnp.max(
        jnp.where(doc_starts <= positions, doc_starts, -first_row), axis=1, keepdims=True
    )
    starts = jnp.broadcast_to(starts, (tok, dim)).T[:1]
    places = lax.broadcasted_iota(jnp.int32, (tok, tok), 0)
    for age in range(SPAN):
        allowed = (places - age * tok).astype(F32) >= starts
        if age == 0:
            allowed = allowed & (places <= lax.broadcasted_iota(jnp.int32, (tok, tok), 1))
        bias[age] = jnp.where(allowed, 0.0, MASKED)

    def of_head(head, count=1):
        return slice(head * tok, (head + count) * tok)

    for copy in head_loads:
        copy.wait()
    for head in range(heads):
        qt[head] = q[of_head(head)].T
        gt[head] = g[of_head(head)].T

    def turn(slot):
        kt[:, of_head(slot)] = kw[slot].T
        vt[:, of_head(slot)] = vw[slot].T

    def folded(values, combine):
        return combine(values.reshape(-1, 8, tok), axis=0)

    def multiply(slot, head, fresh):
        scores = dot(kw[slot], qt[head]) + bias[slot]
        probs[slot, head] = scores
        top = jnp.max(folded(scores, jnp.max), axis=0, keepdims=True)
        if not fresh:
            top = jnp.maximum(row_max[head], top)
        dprobs[slot, head] = dot(vw[slot], gt[head])
        block_max[slot, head] = top

    def weigh(slot, head, fresh):
        top = block_max[slot, head]
        added = jnp.zeros((8, tok), F32)
        dotted = jnp.zeros((8, tok), F32)
        for row in range(0, tok, CHUNK):
            rows = slice(row, row + CHUNK)
            weights = jnp.exp2((probs[slot, head, rows] - top) * to_log2)
            probs[slot, head, rows] = weights
            added += folded(weights, jnp.sum)
            dotted += folded(weights * dprobs[slot, head, rows], jnp.sum)
        added = jnp.sum(added, axis=0, keepdims=True)
        dotted = jnp.sum(dotted, axis=0, keepdims=True)
        if not fresh:
            shrink = jnp.exp2((row_max[head] - top) * to_log2)
            added += row_sum[head] * shrink
            dotted += row_dot[head] * shrink
        row_max[head] = top
        row_sum[head] = added
        row_dot[head] = dotted

    def forward(slot, fresh):
        multiply(slot, 0, fresh)
        for head in range(heads):
            if head + 1 < heads:
                multiply(slot, head + 1, fresh)
            weigh(slot, head, fresh)

    def grade(slot, head):
        whole = 1.0 / row_sum[head]
        delta = row_dot[head] * whole
        scale = jnp.exp2((block_max[slot, head] - row_max[head]) * to_log2) * whole
        for row in range(0, tok, CHUNK):
            rows = slice(row, row + CHUNK)
            there = slice(slot * tok + row, slot * tok + row + CHUNK)
            weights = probs[slot, head, rows] * scale
            low[head, there] = weights.astype(BF16)
            grad_low[head, there] = (weights * (dprobs[slot, head, rows] - delta)).astype(BF16)

    def backward(slot):
        key_sum, value_sum = None, None
        for head in range(GROUP):
            grade(slot, head)
        for first_head in range(0, heads, GROUP):
            group = range(first_head, first_head + GROUP)
            if first_head + GROUP < heads:
                for head in group:
                    grade(slot, head + GROUP)
            side_by_side = [
                jnp.concatenate([ref[head, of_head(slot)] for head in group], axis=1)
                for ref in (grad_low, low)
            ]
            key_part = dot(side_by_side[0], q[of_head(first_head, GROUP)])
            value_part = dot(side_by_side[1], g[of_head(first_head, GROUP)])
            key_sum = key_part if key_sum is None else key_sum + key_part
            value_sum = value_part if value_sum is None else value_sum + value_part
        return key_sum, value_sum

    forward(0, True)

    @pl.when(is_odd & has_relay_target)
    def _():
        for arrived, onward in zip(relay_in, relay_out):
            arrived.wait_recv()
            onward.start()

    @pl.when(is_odd & has_two_before)
    def _():
        for arrived, onward in zip(to_next, passed_to_sibling):
            arrived.wait_recv()
            onward.start()

    @pl.when(is_even & has_two_after)
    def _():
        start(to_next)

    @pl.when(is_odd | has_two_before)
    def _():
        received(own_to_sibling)

    forward(1, False)

    @pl.when(is_even & has_two_before)
    def _():
        received(to_next)
        start(passed_on)

    forward(2, False)

    @pl.when(has_three_before)
    def _():
        received(relay_out)

    forward(3, False)
    key_sum, value_sum = backward(3)
    send_k[0] = key_sum.astype(BF16)
    send_v[0] = value_sum.astype(BF16)

    @pl.when(has_three_before)
    def _():
        start(third)

    key_sum, value_sum = backward(1)
    send_k[1] = key_sum.astype(BF16)
    send_v[1] = value_sum.astype(BF16)

    @pl.when(is_odd | has_two_before)
    def _():
        start(first)

    part_k[1], part_v[1] = backward(2)

    @pl.when(has_two_before)
    def _():
        @pl.when(is_odd)
        def _():
            received(first)

        @pl.when(is_even)
        def _():
            received(third)

        send_k[2] = (part_k[1] + got_k[odd].astype(F32)).astype(BF16)
        send_v[2] = (part_v[1] + got_v[odd].astype(F32)).astype(BF16)
        start(second)

    part_k[0], part_v[0] = backward(0)
    for slot in range(SPAN):
        turn(slot)
    for head in range(heads):
        columns = slice(head * dim, (head + 1) * dim)
        att[:, columns] = dot(vt[...], low[head]).T.astype(BF16)
        dq[:, columns] = (dot(kt[...], grad_low[head]) * score_scale).T.astype(BF16)
    att_copy = pltpu.make_async_copy(att, att_out, out_sem.at[0])
    att_copy.start()
    dq_copy = pltpu.make_async_copy(dq, dq_out, out_sem.at[1])
    dq_copy.start()

    @pl.when(is_even)
    def _():
        received(first)

    @pl.when(is_odd & has_three_after)
    def _():
        received(third)

    part_k[0] += got_k[1 - odd].astype(F32)
    part_v[0] += got_v[1 - odd].astype(F32)

    @pl.when(has_two_after)
    def _():
        received(second)

    dk[...] = ((part_k[0] + got_k[2].astype(F32)) * score_scale).astype(BF16)
    dk_copy = pltpu.make_async_copy(dk, dk_out, out_sem.at[2])
    dk_copy.start()
    dv[...] = (part_v[0] + got_v[2].astype(F32)).astype(BF16)
    dv_copy = pltpu.make_async_copy(dv, dv_out, out_sem.at[3])
    dv_copy.start()

    @pl.when(has_two_after)
    def _():
        sent(to_next)

    @pl.when(is_even | has_two_before)
    def _():
        sent(own_to_sibling)

    @pl.when(is_even & has_two_before)
    def _():
        sent(passed_on)

    @pl.when(is_odd & has_three_after)
    def _():
        sent(relay_in)

    @pl.when(is_odd & has_relay_target)
    def _():
        sent(relay_out)

    @pl.when(has_three_before)
    def _():
        sent(third)

    @pl.when(is_odd | has_two_before)
    def _():
        sent(first)

    @pl.when(has_two_before)
    def _():
        sent(second)

    for copy in (att_copy, dq_copy, dk_copy, dv_copy):
        copy.wait()


def write_out(*refs):
    count = (len(refs) - 1) // 2
    sems = refs[-1]
    copies = [
        pltpu.make_async_copy(refs[i], refs[count + i], sems.at[i]) for i in range(count)
    ]
    for copy in copies:
        copy.start()
    for copy in copies:
        copy.wait()


def local(sizes, queries, key_rows, value_rows, grad_out, doc_starts, doc_ids):
    outer_count, inner_count, tok, heads, dim = sizes
    width = heads * dim
    anywhere = pl.BlockSpec(memory_space=pl.ANY)
    row = (heads, 1, tok)
    shapes = (
        jax.ShapeDtypeStruct((tok, width), BF16),
        jax.ShapeDtypeStruct((tok, width), BF16),
        jax.ShapeDtypeStruct((tok, dim), BF16),
        jax.ShapeDtypeStruct((tok, dim), BF16),
    )
    in_hbm = [
        pltpu.with_memory_space_constraint(x, pltpu.HBM)
        for x in (queries, key_rows, value_rows, grad_out, doc_starts)
    ]
    results = pl.pallas_call(
        functools.partial(kernel, sizes),
        out_shape=tuple(pltpu.VMEM(shape.shape, shape.dtype) for shape in shapes),
        in_specs=[pl.BlockSpec(memory_space=pltpu.HBM)] * 5,
        out_specs=(anywhere,) * 4,
        scratch_shapes=[
            pltpu.VMEM(doc_starts.shape, jnp.int32),
            pltpu.VMEM((heads * tok, dim), BF16),
            pltpu.VMEM((heads * tok, dim), BF16),
            pltpu.VMEM((heads, dim, tok), BF16),
            pltpu.VMEM((heads, dim, tok), BF16),
            pltpu.VMEM((SPAN, tok, dim), BF16),
            pltpu.VMEM((SPAN, tok, dim), BF16),
            pltpu.VMEM((dim, SPAN * tok), BF16),
            pltpu.VMEM((dim, SPAN * tok), BF16),
            pltpu.VMEM((SPAN, tok, tok), F32),
            pltpu.VMEM((SPAN, heads, tok, tok), F32),
            pltpu.VMEM((SPAN, heads, tok, tok), F32),
            pltpu.VMEM((heads, SPAN * tok, tok), BF16),
            pltpu.VMEM((heads, SPAN * tok, tok), BF16),
            pltpu.VMEM(row, F32),
            pltpu.VMEM(row, F32),
            pltpu.VMEM(row, F32),
            pltpu.VMEM((SPAN,) + row, F32),
            pltpu.VMEM((tok, dim), BF16),
            pltpu.VMEM((tok, dim), BF16),
            pltpu.VMEM((2, tok, dim), F32),
            pltpu.VMEM((2, tok, dim), F32),
            pltpu.VMEM((SPAN - 1, tok, dim), BF16),
            pltpu.VMEM((SPAN - 1, tok, dim), BF16),
            pltpu.VMEM((SPAN - 1, tok, dim), BF16),
            pltpu.VMEM((SPAN - 1, tok, dim), BF16),
            pltpu.VMEM((tok, width), BF16),
            pltpu.VMEM((tok, width), BF16),
            pltpu.VMEM((tok, dim), BF16),
            pltpu.VMEM((tok, dim), BF16),
            pltpu.SemaphoreType.DMA((3 + 2 * heads,)),
            pltpu.SemaphoreType.DMA((4,)),
            pltpu.SemaphoreType.DMA((14,)),
            pltpu.SemaphoreType.DMA((14,)),
        ],
        compiler_params=pltpu.CompilerParams(
            collective_id=0, has_side_effects=True, vmem_limit_bytes=VMEM_BYTES
        ),
        cost_estimate=pl.CostEstimate(
            flops=12 * tok * heads * SPAN * tok * dim,
            bytes_accessed=8 * tok * (width + dim),
            transcendentals=SPAN * tok * tok * heads,
        ),
    )(*in_hbm)
    return pl.pallas_call(
        write_out,
        out_shape=shapes,
        in_specs=[anywhere] * 4,
        out_specs=(anywhere,) * 4,
        scratch_shapes=[pltpu.SemaphoreType.DMA((4,))],
        compiler_params=pltpu.CompilerParams(vmem_limit_bytes=VMEM_BYTES),
    )(*results)


def solution(mesh):
    rows = P(("outer", "inner"), None)

    def program(queries, key_rows, value_rows, grad_out, doc_starts, doc_ids):
        outer_count, inner_count = mesh.shape["outer"], mesh.shape["inner"]
        dim = key_rows.shape[1]
        sizes = (
            outer_count,
            inner_count,
            key_rows.shape[0] // (outer_count * inner_count),
            queries.shape[1] // dim,
            dim,
        )
        return jax.shard_map(
            functools.partial(local, sizes),
            mesh=mesh,
            in_specs=(rows, rows, rows, rows, P(), P(("outer", "inner"))),
            out_specs=(rows, rows, rows, rows),
            check_vma=False,
        )(queries, key_rows, value_rows, grad_out, doc_starts, doc_ids)

    return program
```

time: 183 us -> 37.7 us (0.21)
  the two profiles are of different devices: /device:TPU:21 before, /device:TPU:28 now
where the time goes in v1:
time: 37.7 us; the launch traced here: 37.5 us
  Pallas kernels  36.8 us (98%)
  between operations  0.64 us (2%)
    pallas_call x1, Pallas kernels, local(): pl.pallas_call(functools.partial(kernel, sizes), out_shape=tuple((pltpu.V...  35.8 us
    pallas_call x1, Pallas kernels, local(): pl.pallas_call(write_out, out_shape=shapes, in_specs=[anywhere] * 4, out_...  1.03 us

profile of v1, /device:TPU:28, one launch (start us, length us, event | category | flops | bytes accessed | tf_op | source)
XLA Modules:
  0.0 37.5 jit_solution(1777178028946706212)
XLA Ops:
  0.6 35.8 %shard_map.84 = (bf16[256,1024]{1,0:T(8,128)(2,1)S(1)}, bf16[256,1024]{1,0:T(8,128)(2,1)S(1)}, bf16[256,128]{1,0:T(8,128)(2,1)S(1)}, bf16[256,128]{1,0:T(8,128)(2,1)S(1)}) custom-call(bf16[256,1024]{1,0:T(8,128)(2,1)} %q_in.1, bf16[256,128]{1,0:T(8,128)(2,1)} %k_in.1, bf16[256,128]{1,0:T(8,128)(2,1)} %v_in.1, bf16[256,1024]{1,0:T(8,128)(2,1)} %g_in.1, s32[341]{0:T(512)} %doc_in.1), custom_call_target="tpu_custom_call" | custom-call | flops 3221225472 | bytes 2359296 | tf_op jit(solution)/shard_map/pallas_call | solution.py:436
  36.4 1.0 %shard_map.85 = (bf16[256,1024]{1,0:T(8,128)(2,1)}, bf16[256,1024]{1,0:T(8,128)(2,1)}, bf16[256,128]{1,0:T(8,128)(2,1)}, bf16[256,128]{1,0:T(8,128)(2,1)}) custom-call(bf16[256,1024]{1,0:T(8,128)(2,1)S(1)} %get-tuple-element.8.refs_0_, bf16[256,1024]{1,0:T(8,128)(2,1)S(1)} %get-tuple-element.9.refs_1_, bf16[256,128]{1,0:T(8,128)(2,1)S(1)} %get-tuple-element.10.refs_2_, ...), custom_call_target="tpu_custom_call" | custom-call | tf_op jit(solution)/shard_map/pallas_call | solution.py:486

commit v2 on v1

--- a/solution.py
+++ b/solution.py
@@ -12,6 +12,7 @@
 SPAN = 4
 CHUNK = 32
 GROUP = 2
+UNROLL = 4
 MASKED = -1e30
 VMEM_BYTES = 48 * 2**20
 F32 = jnp.float32
@@ -27,7 +28,7 @@
     q_in, k_in, v_in, g_in, doc_in,
     att_out, dq_out, dk_out, dv_out,
     docs, q, g, qt, gt, kw, vw, kt, vt, bias, probs, dprobs, low, grad_low, row_max, row_sum, row_dot, block_max,
-    relay_k, relay_v, part_k, part_v, send_k, send_v, got_k, got_v, att, dq, dk, dv,
+    relay_k, relay_v, key_sum, value_sum, send_k, send_v, got_k, got_v, att, dq, dk, dv,
     local_sem, out_sem, send_sem, recv_sem,
 ):
     outer_count, inner_count, tok, heads, dim = sizes
@@ -187,31 +188,33 @@
         bias[age] = jnp.where(allowed, 0.0, MASKED)
 
     def of_head(head, count=1):
-        return slice(head * tok, (head + count) * tok)
+        return pl.ds(pl.multiple_of(head * tok, tok), count * tok)
 
     for copy in head_loads:
         copy.wait()
-    for head in range(heads):
-        qt[head] = q[of_head(head)].T
-        gt[head] = g[of_head(head)].T
-
-    def turn(slot):
-        kt[:, of_head(slot)] = kw[slot].T
-        vt[:, of_head(slot)] = vw[slot].T
+
+    @pl.loop(0, heads // UNROLL)
+    def _(part):
+        for offset in range(UNROLL):
+            head = part * UNROLL + offset
+            qt[head] = q[of_head(head)].T
+            gt[head] = g[of_head(head)].T
+
+    row_max[...] = jnp.full_like(row_max, MASKED)
+    row_sum[...] = jnp.zeros_like(row_sum)
+    row_dot[...] = jnp.zeros_like(row_dot)
 
     def folded(values, combine):
         return combine(values.reshape(-1, 8, tok), axis=0)
 
-    def multiply(slot, head, fresh):
+    def multiply(slot, head):
         scores = dot(kw[slot], qt[head]) + bias[slot]
         probs[slot, head] = scores
         top = jnp.max(folded(scores, jnp.max), axis=0, keepdims=True)
-        if not fresh:
-            top = jnp.maximum(row_max[head], top)
         dprobs[slot, head] = dot(vw[slot], gt[head])
-        block_max[slot, head] = top
-
-    def weigh(slot, head, fresh):
+        block_max[slot, head] = jnp.maximum(row_max[head], top)
+
+    def weigh(slot, head):
         top = block_max[slot, head]
         added = jnp.zeros((8, tok), F32)
         dotted = jnp.zeros((8, tok), F32)
@@ -221,22 +224,10 @@
             probs[slot, head, rows] = weights
             added += folded(weights, jnp.sum)
             dotted += folded(weights * dprobs[slot, head, rows], jnp.sum)
-        added = jnp.sum(added, axis=0, keepdims=True)
-        dotted = jnp.sum(dotted, axis=0, keepdims=True)
-        if not fresh:
-            shrink = jnp.exp2((row_max[head] - top) * to_log2)
-            added += row_sum[head] * shrink
-            dotted += row_dot[head] * shrink
+        shrink = jnp.exp2((row_max[head] - top) * to_log2)
         row_max[head] = top
-        row_sum[head] = added
-        row_dot[head] = dotted
-
-    def forward(slot, fresh):
-        multiply(slot, 0, fresh)
-        for head in range(heads):
-            if head + 1 < heads:
-                multiply(slot, head + 1, fresh)
-            weigh(slot, head, fresh)
+        row_sum[head] = row_sum[head] * shrink + jnp.sum(added, axis=0, keepdims=True)
+        row_dot[head] = row_dot[head] * shrink + jnp.sum(dotted, axis=0, keepdims=True)
 
     def grade(slot, head):
         whole = 1.0 / row_sum[head]
@@ -244,105 +235,118 @@
         scale = jnp.exp2((block_max[slot, head] - row_max[head]) * to_log2) * whole
         for row in range(0, tok, CHUNK):
             rows = slice(row, row + CHUNK)
-            there = slice(slot * tok + row, slot * tok + row + CHUNK)
             weights = probs[slot, head, rows] * scale
-            low[head, there] = weights.astype(BF16)
-            grad_low[head, there] = (weights * (dprobs[slot, head, rows] - delta)).astype(BF16)
-
-    def backward(slot):
-        key_sum, value_sum = None, None
-        for head in range(GROUP):
-            grade(slot, head)
-        for first_head in range(0, heads, GROUP):
-            group = range(first_head, first_head + GROUP)
-            if first_head + GROUP < heads:
+            low[head, slot, rows] = weights.astype(BF16)
+            grad_low[head, slot, rows] = (
+                weights * (dprobs[slot, head, rows] - delta)
+            ).astype(BF16)
+
+    @pl.loop(0, SPAN)
+    def _(slot):
+        @pl.when(slot == 1)
+        def _():
+            @pl.when(is_odd & has_relay_target)
+            def _():
+                for arrived, onward in zip(relay_in, relay_out):
+                    arrived.wait_recv()
+                    onward.start()
+
+            @pl.when(is_odd & has_two_before)
+            def _():
+                for arrived, onward in zip(to_next, passed_to_sibling):
+                    arrived.wait_recv()
+                    onward.start()
+
+            @pl.when(is_even & has_two_after)
+            def _():
+                start(to_next)
+
+            @pl.when(is_odd | has_two_before)
+            def _():
+                received(own_to_sibling)
+
+        @pl.when((slot == 2) & is_even & has_two_before)
+        def _():
+            received(to_next)
+            start(passed_on)
+
+        @pl.when((slot == 3) & has_three_before)
+        def _():
+            received(relay_out)
+
+        @pl.loop(0, heads // UNROLL)
+        def _(part):
+            group = [part * UNROLL + offset for offset in range(UNROLL)]
+            multiply(slot, group[0])
+            for place, head in enumerate(group):
+                if place + 1 < UNROLL:
+                    multiply(slot, group[place + 1])
+                weigh(slot, head)
+
+    @pl.loop(0, SPAN)
+    def _(turn):
+        slot = jnp.where(turn == 0, 3, jnp.where(turn == 3, 0, turn))
+        key_sum[...] = jnp.zeros_like(key_sum)
+        value_sum[...] = jnp.zeros_like(value_sum)
+
+        @pl.loop(0, heads // UNROLL)
+        def _(part):
+            keys, values = key_sum[...], value_sum[...]
+            for pair_place in range(0, UNROLL, GROUP):
+                first_head = part * UNROLL + pair_place
+                group = [first_head + offset for offset in range(GROUP)]
                 for head in group:
-                    grade(slot, head + GROUP)
-            side_by_side = [
-                jnp.concatenate([ref[head, of_head(slot)] for head in group], axis=1)
-                for ref in (grad_low, low)
-            ]
-            key_part = dot(side_by_side[0], q[of_head(first_head, GROUP)])
-            value_part = dot(side_by_side[1], g[of_head(first_head, GROUP)])
-            key_sum = key_part if key_sum is None else key_sum + key_part
-            value_sum = value_part if value_sum is None else value_sum + value_part
-        return key_sum, value_sum
-
-    forward(0, True)
-
-    @pl.when(is_odd & has_relay_target)
-    def _():
-        for arrived, onward in zip(relay_in, relay_out):
-            arrived.wait_recv()
-            onward.start()
-
-    @pl.when(is_odd & has_two_before)
-    def _():
-        for arrived, onward in zip(to_next, passed_to_sibling):
-            arrived.wait_recv()
-            onward.start()
-
-    @pl.when(is_even & has_two_after)
-    def _():
-        start(to_next)
-
-    @pl.when(is_odd | has_two_before)
-    def _():
-        received(own_to_sibling)
-
-    forward(1, False)
-
-    @pl.when(is_even & has_two_before)
-    def _():
-        received(to_next)
-        start(passed_on)
-
-    forward(2, False)
-
-    @pl.when(has_three_before)
-    def _():
-        received(relay_out)
-
-    forward(3, False)
-    key_sum, value_sum = backward(3)
-    send_k[0] = key_sum.astype(BF16)
-    send_v[0] = value_sum.astype(BF16)
-
-    @pl.when(has_three_before)
-    def _():
-        start(third)
-
-    key_sum, value_sum = backward(1)
-    send_k[1] = key_sum.astype(BF16)
-    send_v[1] = value_sum.astype(BF16)
-
-    @pl.when(is_odd | has_two_before)
-    def _():
-        start(first)
-
-    part_k[1], part_v[1] = backward(2)
-
-    @pl.when(has_two_before)
-    def _():
-        @pl.when(is_odd)
+                    grade(slot, head)
+                side_by_side = [
+                    jnp.concatenate([ref[head, slot] for head in group], axis=1)
+                    for ref in (grad_low, low)
+                ]
+                keys += dot(side_by_side[0], q[of_head(first_head, GROUP)])
+                values += dot(side_by_side[1], g[of_head(first_head, GROUP)])
+            key_sum[...] = keys
+            value_sum[...] = values
+
+        @pl.when((turn == 0) & has_three_before)
         def _():
-            received(first)
-
-        @pl.when(is_even)
+            send_k[0] = key_sum[...].astype(BF16)
+            send_v[0] = value_sum[...].astype(BF16)
+            start(third)
+
+        @pl.when((turn == 1) & (is_odd | has_two_before))
         def _():
-            received(third)
-
-        send_k[2] = (part_k[1] + got_k[odd].astype(F32)).astype(BF16)
-        send_v[2] = (part_v[1] + got_v[odd].astype(F32)).astype(BF16)
-        start(second)
-
-    part_k[0], part_v[0] = backward(0)
+            send_k[1] = key_sum[...].astype(BF16)
+            send_v[1] = value_sum[...].astype(BF16)
+            start(first)
+
+        @pl.when((turn == 2) & has_two_before)
+        def _():
+            @pl.when(is_odd)
+            def _():
+                received(first)
+
+            @pl.when(is_even)
+            def _():
+                received(third)
+
+            send_k[2] = (key_sum[...] + got_k[odd].astype(F32)).astype(BF16)
+            send_v[2] = (value_sum[...] + got_v[odd].astype(F32)).astype(BF16)
+            start(second)
+
     for slot in range(SPAN):
-        turn(slot)
-    for head in range(heads):
-        columns = slice(head * dim, (head + 1) * dim)
-        att[:, columns] = dot(vt[...], low[head]).T.astype(BF16)
-        dq[:, columns] = (dot(kt[...], grad_low[head]) * score_scale).T.astype(BF16)
+        columns = slice(slot * tok, (slot + 1) * tok)
+        kt[:, columns] = kw[slot].T
+        vt[:, columns] = vw[slot].T
+
+    @pl.loop(0, heads // GROUP)
+    def _(part):
+        for offset in range(GROUP):
+            head = part * GROUP + offset
+            columns = pl.ds(pl.multiple_of(head * dim, dim), dim)
+            weights = low[head].reshape(SPAN * tok, tok)
+            grads = grad_low[head].reshape(SPAN * tok, tok)
+            att[:, columns] = dot(vt[...], weights).T.astype(BF16)
+            dq[:, columns] = (dot(kt[...], grads) * score_scale).T.astype(BF16)
+
     att_copy = pltpu.make_async_copy(att, att_out, out_sem.at[0])
     att_copy.start()
     dq_copy = pltpu.make_async_copy(dq, dq_out, out_sem.at[1])
@@ -356,17 +360,17 @@
     def _():
         received(third)
 
-    part_k[0] += got_k[1 - odd].astype(F32)
-    part_v[0] += got_v[1 - odd].astype(F32)
+    key_sum[...] += got_k[1 - odd].astype(F32)
+    value_sum[...] += got_v[1 - odd].astype(F32)
 
     @pl.when(has_two_after)
     def _():
         received(second)
 
-    dk[...] = ((part_k[0] + got_k[2].astype(F32)) * score_scale).astype(BF16)
+    dk[...] = ((key_sum[...] + got_k[2].astype(F32)) * score_scale).astype(BF16)
     dk_copy = pltpu.make_async_copy(dk, dk_out, out_sem.at[2])
     dk_copy.start()
-    dv[...] = (part_v[0] + got_v[2].astype(F32)).astype(BF16)
+    dv[...] = (value_sum[...] + got_v[2].astype(F32)).astype(BF16)
     dv_copy = pltpu.make_async_copy(dv, dv_out, out_sem.at[3])
     dv_copy.start()
 
@@ -451,16 +455,16 @@
             pltpu.VMEM((SPAN, tok, tok), F32),
             pltpu.VMEM((SPAN, heads, tok, tok), F32),
             pltpu.VMEM((SPAN, heads, tok, tok), F32),
-            pltpu.VMEM((heads, SPAN * tok, tok), BF16),
-            pltpu.VMEM((heads, SPAN * tok, tok), BF16),
+            pltpu.VMEM((heads, SPAN, tok, tok), BF16),
+            pltpu.VMEM((heads, SPAN, tok, tok), BF16),
             pltpu.VMEM(row, F32),
             pltpu.VMEM(row, F32),
             pltpu.VMEM(row, F32),
             pltpu.VMEM((SPAN,) + row, F32),
             pltpu.VMEM((tok, dim), BF16),
             pltpu.VMEM((tok, dim), BF16),
-            pltpu.VMEM((2, tok, dim), F32),
-            pltpu.VMEM((2, tok, dim), F32),
+            pltpu.VMEM((tok, dim), F32),
+            pltpu.VMEM((tok, dim), F32),
             pltpu.VMEM((SPAN - 1, tok, dim), BF16),
             pltpu.VMEM((SPAN - 1, tok, dim), BF16),
             pltpu.VMEM((SPAN - 1, tok, dim), BF16),

time: 37.7 us -> 38.5 us (1.021)
  Pallas kernels: 36.8 us -> 37.7 us
    pallas_call x1, Pallas kernels: 35.8 us -> 36.7 us  [local(): pl.pallas_call(functools.partial(kernel, sizes), out_shape=tuple((pltpu.V...]
where the time goes in v2:
time: 38.5 us; the launch traced here: 38.3 us
  Pallas kernels  37.7 us (98%)
  between operations  0.64 us (2%)
    pallas_call x1, Pallas kernels, local(): pl.pallas_call(functools.partial(kernel, sizes), out_shape=tuple((pltpu.V...  36.7 us
    pallas_call x1, Pallas kernels, local(): pl.pallas_call(write_out, out_shape=shapes, in_specs=[anywhere] * 4, out_...  1.03 us

profile of v2, /device:TPU:28, one launch (start us, length us, event | category | flops | bytes accessed | tf_op | source)
XLA Modules:
  0.0 38.3 jit_solution(11003398434081353553)
XLA Ops:
  0.6 36.7 %shard_map.84 = (bf16[256,1024]{1,0:T(8,128)(2,1)S(1)}, bf16[256,1024]{1,0:T(8,128)(2,1)S(1)}, bf16[256,128]{1,0:T(8,128)(2,1)S(1)}, bf16[256,128]{1,0:T(8,128)(2,1)S(1)}) custom-call(bf16[256,1024]{1,0:T(8,128)(2,1)} %q_in.1, bf16[256,128]{1,0:T(8,128)(2,1)} %k_in.1, bf16[256,128]{1,0:T(8,128)(2,1)} %v_in.1, bf16[256,1024]{1,0:T(8,128)(2,1)} %g_in.1, s32[341]{0:T(512)} %doc_in.1), custom_call_target="tpu_custom_call" | custom-call | flops 3221225472 | bytes 2359296 | tf_op jit(solution)/shard_map/pallas_call | solution.py:440
  37.3 1.0 %shard_map.85 = (bf16[256,1024]{1,0:T(8,128)(2,1)}, bf16[256,1024]{1,0:T(8,128)(2,1)}, bf16[256,128]{1,0:T(8,128)(2,1)}, bf16[256,128]{1,0:T(8,128)(2,1)}) custom-call(bf16[256,1024]{1,0:T(8,128)(2,1)S(1)} %get-tuple-element.8.refs_0_, bf16[256,1024]{1,0:T(8,128)(2,1)S(1)} %get-tuple-element.9.refs_1_, bf16[256,128]{1,0:T(8,128)(2,1)S(1)} %get-tuple-element.10.refs_2_, ...), custom_call_target="tpu_custom_call" | custom-call | tf_op jit(solution)/shard_map/pallas_call | solution.py:490

commit v3 on v2

--- a/solution.py
+++ b/solution.py
@@ -12,7 +12,7 @@
 SPAN = 4
 CHUNK = 32
 GROUP = 2
-UNROLL = 4
+UNROLL = 8
 MASKED = -1e30
 VMEM_BYTES = 48 * 2**20
 F32 = jnp.float32
@@ -26,10 +26,10 @@
 def kernel(
     sizes,
     q_in, k_in, v_in, g_in, doc_in,
-    att_out, dq_out, dk_out, dv_out,
+    att, dq, dk, dv,
     docs, q, g, qt, gt, kw, vw, kt, vt, bias, probs, dprobs, low, grad_low, row_max, row_sum, row_dot, block_max,
-    relay_k, relay_v, key_sum, value_sum, send_k, send_v, got_k, got_v, att, dq, dk, dv,
-    local_sem, out_sem, send_sem, recv_sem,
+    relay_k, relay_v, key_sum, value_sum, send_k, send_v, got_k, got_v,
+    local_sem, send_sem, recv_sem,
 ):
     outer_count, inner_count, tok, heads, dim = sizes
     total = outer_count * inner_count
@@ -153,25 +153,6 @@
         for copy in copies:
             copy.wait_send()
 
-    key_load.wait()
-    value_load.wait()
-    targets = 1 + jnp.where(has_two_after, 1, 0)
-    targets += jnp.where(is_odd & has_three_after, 1, 0)
-    targets += jnp.where(is_odd & has_relay_target, 1, 0)
-    pl.semaphore_wait(barrier, targets)
-
-    @pl.when(is_even)
-    def _():
-        start(own_to_sibling)
-
-    @pl.when(is_odd & has_two_after)
-    def _():
-        start(to_next)
-
-    @pl.when(is_odd & has_three_after)
-    def _():
-        start(relay_in)
-
     doc_load.wait()
     first_row = (me * tok).astype(F32)
     doc_starts = jnp.broadcast_to(docs[...][None, :].astype(F32), (tok, docs.shape[0])) - first_row
@@ -187,6 +168,25 @@
             allowed = allowed & (places <= lax.broadcasted_iota(jnp.int32, (tok, tok), 1))
         bias[age] = jnp.where(allowed, 0.0, MASKED)
 
+    key_load.wait()
+    value_load.wait()
+    targets = 1 + jnp.where(has_two_after, 1, 0)
+    targets += jnp.where(is_odd & has_three_after, 1, 0)
+    targets += jnp.where(is_odd & has_relay_target, 1, 0)
+    pl.semaphore_wait(barrier, targets)
+
+    @pl.when(is_even)
+    def _():
+        start(own_to_sibling)
+
+    @pl.when(is_odd & has_two_after)
+    def _():
+        start(to_next)
+
+    @pl.when(is_odd & has_three_after)
+    def _():
+        start(relay_in)
+
     def of_head(head, count=1):
         return pl.ds(pl.multiple_of(head * tok, tok), count * tok)
 
@@ -200,45 +200,51 @@
             qt[head] = q[of_head(head)].T
             gt[head] = g[of_head(head)].T
 
-    row_max[...] = jnp.full_like(row_max, MASKED)
-    row_sum[...] = jnp.zeros_like(row_sum)
-    row_dot[...] = jnp.zeros_like(row_dot)
+    @pl.when(is_even & has_two_after)
+    def _():
+        start(to_next)
+
+    for place in range(UNROLL):
+        row_max[place][...] = jnp.full(row_max[place].shape, MASKED, F32)
+        row_sum[place][...] = jnp.zeros(row_sum[place].shape, F32)
+        row_dot[place][...] = jnp.zeros(row_dot[place].shape, F32)
 
     def folded(values, combine):
         return combine(values.reshape(-1, 8, tok), axis=0)
 
-    def multiply(slot, head):
+    def multiply(slot, part, place):
+        head = part * UNROLL + place
         scores = dot(kw[slot], qt[head]) + bias[slot]
-        probs[slot, head] = scores
+        probs[place][slot, part] = scores
         top = jnp.max(folded(scores, jnp.max), axis=0, keepdims=True)
-        dprobs[slot, head] = dot(vw[slot], gt[head])
-        block_max[slot, head] = jnp.maximum(row_max[head], top)
-
-    def weigh(slot, head):
-        top = block_max[slot, head]
+        dprobs[place][slot, part] = dot(vw[slot], gt[head])
+        return jnp.maximum(row_max[place][part], top)
+
+    def weigh(slot, part, place, top):
         added = jnp.zeros((8, tok), F32)
         dotted = jnp.zeros((8, tok), F32)
         for row in range(0, tok, CHUNK):
             rows = slice(row, row + CHUNK)
-            weights = jnp.exp2((probs[slot, head, rows] - top) * to_log2)
-            probs[slot, head, rows] = weights
+            weights = jnp.exp2((probs[place][slot, part, rows] - top) * to_log2)
+            probs[place][slot, part, rows] = weights
             added += folded(weights, jnp.sum)
-            dotted += folded(weights * dprobs[slot, head, rows], jnp.sum)
-        shrink = jnp.exp2((row_max[head] - top) * to_log2)
-        row_max[head] = top
-        row_sum[head] = row_sum[head] * shrink + jnp.sum(added, axis=0, keepdims=True)
-        row_dot[head] = row_dot[head] * shrink + jnp.sum(dotted, axis=0, keepdims=True)
-
-    def grade(slot, head):
-        whole = 1.0 / row_sum[head]
-        delta = row_dot[head] * whole
-        scale = jnp.exp2((block_max[slot, head] - row_max[head]) * to_log2) * whole
+            dotted += folded(weights * dprobs[place][slot, part, rows], jnp.sum)
+        shrink = jnp.exp2((row_max[place][part] - top) * to_log2)
+        block_max[place][slot, part] = top
+        row_max[place][part] = top
+        row_sum[place][part] = row_sum[place][part] * shrink + jnp.sum(added, axis=0, keepdims=True)
+        row_dot[place][part] = row_dot[place][part] * shrink + jnp.sum(dotted, axis=0, keepdims=True)
+
+    def grade(slot, part, place):
+        whole = 1.0 / row_sum[place][part]
+        delta = row_dot[place][part] * whole
+        scale = jnp.exp2((block_max[place][slot, part] - row_max[place][part]) * to_log2) * whole
         for row in range(0, tok, CHUNK):
             rows = slice(row, row + CHUNK)
-            weights = probs[slot, head, rows] * scale
-            low[head, slot, rows] = weights.astype(BF16)
-            grad_low[head, slot, rows] = (
-                weights * (dprobs[slot, head, rows] - delta)
+            weights = probs[place][slot, part, rows] * scale
+            low[place][part, slot, rows] = weights.astype(BF16)
+            grad_low[place][part, slot, rows] = (
+                weights * (dprobs[place][slot, part, rows] - delta)
             ).astype(BF16)
 
     @pl.loop(0, SPAN)
@@ -257,10 +263,6 @@
                     arrived.wait_recv()
                     onward.start()
 
-            @pl.when(is_even & has_two_after)
-            def _():
-                start(to_next)
-
             @pl.when(is_odd | has_two_before)
             def _():
                 received(own_to_sibling)
@@ -276,49 +278,52 @@
 
         @pl.loop(0, heads // UNROLL)
         def _(part):
-            group = [part * UNROLL + offset for offset in range(UNROLL)]
-            multiply(slot, group[0])
-            for place, head in enumerate(group):
+            tops = [multiply(slot, part, 0)]
+            for place in range(UNROLL):
                 if place + 1 < UNROLL:
-                    multiply(slot, group[place + 1])
-                weigh(slot, head)
+                    tops.append(multiply(slot, part, place + 1))
+                weigh(slot, part, place, tops[place])
 
     @pl.loop(0, SPAN)
     def _(turn):
-        slot = jnp.where(turn == 0, 3, jnp.where(turn == 3, 0, turn))
+        even_slot = jnp.where(turn == 0, 1, jnp.where(turn == 1, 3, 2))
+        slot = jnp.where(turn == 3, 0, jnp.where(is_odd, 3 - turn, even_slot))
         key_sum[...] = jnp.zeros_like(key_sum)
         value_sum[...] = jnp.zeros_like(value_sum)
 
         @pl.loop(0, heads // UNROLL)
         def _(part):
             keys, values = key_sum[...], value_sum[...]
-            for pair_place in range(0, UNROLL, GROUP):
-                first_head = part * UNROLL + pair_place
-                group = [first_head + offset for offset in range(GROUP)]
-                for head in group:
-                    grade(slot, head)
+            for place in range(GROUP):
+                grade(slot, part, place)
+            for first in range(0, UNROLL, GROUP):
+                group = range(first, first + GROUP)
+                if first + GROUP < UNROLL:
+                    for place in group:
+                        grade(slot, part, place + GROUP)
                 side_by_side = [
-                    jnp.concatenate([ref[head, slot] for head in group], axis=1)
+                    jnp.concatenate([ref[place][part, slot] for place in group], axis=1)
                     for ref in (grad_low, low)
                 ]
-                keys += dot(side_by_side[0], q[of_head(first_head, GROUP)])
-                values += dot(side_by_side[1], g[of_head(first_head, GROUP)])
+                rows = of_head(part * UNROLL + first, GROUP)
+                keys += dot(side_by_side[0], q[rows])
+                values += dot(side_by_side[1], g[rows])
             key_sum[...] = keys
             value_sum[...] = values
 
-        @pl.when((turn == 0) & has_three_before)
+        @pl.when((slot == 3) & has_three_before)
         def _():
             send_k[0] = key_sum[...].astype(BF16)
             send_v[0] = value_sum[...].astype(BF16)
             start(third)
 
-        @pl.when((turn == 1) & (is_odd | has_two_before))
+        @pl.when((slot == 1) & (is_odd | has_two_before))
         def _():
             send_k[1] = key_sum[...].astype(BF16)
             send_v[1] = value_sum[...].astype(BF16)
             start(first)
 
-        @pl.when((turn == 2) & has_two_before)
+        @pl.when((slot == 2) & has_two_before)
         def _():
             @pl.when(is_odd)
             def _():
@@ -337,21 +342,15 @@
         kt[:, columns] = kw[slot].T
         vt[:, columns] = vw[slot].T
 
-    @pl.loop(0, heads // GROUP)
+    @pl.loop(0, heads // UNROLL)
     def _(part):
-        for offset in range(GROUP):
-            head = part * GROUP + offset
-            columns = pl.ds(pl.multiple_of(head * dim, dim), dim)
-            weights = low[head].reshape(SPAN * tok, tok)
-            grads = grad_low[head].reshape(SPAN * tok, tok)
+        for place in range(UNROLL):
+            columns = pl.ds(pl.multiple_of((part * UNROLL + place) * dim, dim), dim)
+            weights = low[place][part].reshape(SPAN * tok, tok)
+            grads = grad_low[place][part].reshape(SPAN * tok, tok)
             att[:, columns] = dot(vt[...], weights).T.astype(BF16)
             dq[:, columns] = (dot(kt[...], grads) * score_scale).T.astype(BF16)
 
-    att_copy = pltpu.make_async_copy(att, att_out, out_sem.at[0])
-    att_copy.start()
-    dq_copy = pltpu.make_async_copy(dq, dq_out, out_sem.at[1])
-    dq_copy.start()
-
     @pl.when(is_even)
     def _():
         received(first)
@@ -368,11 +367,7 @@
         received(second)
 
     dk[...] = ((key_sum[...] + got_k[2].astype(F32)) * score_scale).astype(BF16)
-    dk_copy = pltpu.make_async_copy(dk, dk_out, out_sem.at[2])
-    dk_copy.start()
     dv[...] = (value_sum[...] + got_v[2].astype(F32)).astype(BF16)
-    dv_copy = pltpu.make_async_copy(dv, dv_out, out_sem.at[3])
-    dv_copy.start()
 
     @pl.when(has_two_after)
     def _():
@@ -405,9 +400,6 @@
     @pl.when(has_two_before)
     def _():
         sent(second)
-
-    for copy in (att_copy, dq_copy, dk_copy, dv_copy):
-        copy.wait()
 
 
 def write_out(*refs):
@@ -426,7 +418,8 @@
     outer_count, inner_count, tok, heads, dim = sizes
     width = heads * dim
     anywhere = pl.BlockSpec(memory_space=pl.ANY)
-    row = (heads, 1, tok)
+    parts = heads // UNROLL
+    row = (parts, 1, tok)
     shapes = (
         jax.ShapeDtypeStruct((tok, width), BF16),
         jax.ShapeDtypeStruct((tok, width), BF16),
@@ -441,7 +434,7 @@
         functools.partial(kernel, sizes),
         out_shape=tuple(pltpu.VMEM(shape.shape, shape.dtype) for shape in shapes),
         in_specs=[pl.BlockSpec(memory_space=pltpu.HBM)] * 5,
-        out_specs=(anywhere,) * 4,
+        out_specs=(pl.BlockSpec(memory_space=pltpu.VMEM),) * 4,
         scratch_shapes=[
             pltpu.VMEM(doc_starts.shape, jnp.int32),
             pltpu.VMEM((heads * tok, dim), BF16),
@@ -453,14 +446,14 @@
             pltpu.VMEM((dim, SPAN * tok), BF16),
             pltpu.VMEM((dim, SPAN * tok), BF16),
             pltpu.VMEM((SPAN, tok, tok), F32),
-            pltpu.VMEM((SPAN, heads, tok, tok), F32),
-            pltpu.VMEM((SPAN, heads, tok, tok), F32),
-            pltpu.VMEM((heads, SPAN, tok, tok), BF16),
-            pltpu.VMEM((heads, SPAN, tok, tok), BF16),
-            pltpu.VMEM(row, F32),
-            pltpu.VMEM(row, F32),
-            pltpu.VMEM(row, F32),
-            pltpu.VMEM((SPAN,) + row, F32),
+            [pltpu.VMEM((SPAN, parts, tok, tok), F32)] * UNROLL,
+            [pltpu.VMEM((SPAN, parts, tok, tok), F32)] * UNROLL,
+            [pltpu.VMEM((parts, SPAN, tok, tok), BF16)] * UNROLL,
+            [pltpu.VMEM((parts, SPAN, tok, tok), BF16)] * UNROLL,
+            [pltpu.VMEM(row, F32)] * UNROLL,
+            [pltpu.VMEM(row, F32)] * UNROLL,
+            [pltpu.VMEM(row, F32)] * UNROLL,
+            [pltpu.VMEM((SPAN,) + row, F32)] * UNROLL,
             pltpu.VMEM((tok, dim), BF16),
             pltpu.VMEM((tok, dim), BF16),
             pltpu.VMEM((tok, dim), F32),
@@ -469,12 +462,7 @@
             pltpu.VMEM((SPAN - 1, tok, dim), BF16),
             pltpu.VMEM((SPAN - 1, tok, dim), BF16),
             pltpu.VMEM((SPAN - 1, tok, dim), BF16),
-            pltpu.VMEM((tok, width), BF16),
-            pltpu.VMEM((tok, width), BF16),
-            pltpu.VMEM((tok, dim), BF16),
-            pltpu.VMEM((tok, dim), BF16),
             pltpu.SemaphoreType.DMA((3 + 2 * heads,)),
-            pltpu.SemaphoreType.DMA((4,)),
             pltpu.SemaphoreType.DMA((14,)),
             pltpu.SemaphoreType.DMA((14,)),
         ],

time: 38.5 us -> 38 us (0.987)
  the two profiles are of different devices: /device:TPU:28 before, /device:TPU:5 now
where the time goes in v3:
time: 38 us; the launch traced here: 37.8 us
  Pallas kernels  37.2 us (98%)
  between operations  0.64 us (2%)
    pallas_call x1, Pallas kernels, local(): pl.pallas_call(functools.partial(kernel, sizes), out_shape=tuple((pltpu.V...  36.2 us
    pallas_call x1, Pallas kernels, local(): pl.pallas_call(write_out, out_shape=shapes, in_specs=[anywhere] * 4, out_...  1.03 us

profile of v3, /device:TPU:5, one launch (start us, length us, event | category | flops | bytes accessed | tf_op | source)
XLA Modules:
  0.0 37.8 jit_solution(6452404069788648290)
XLA Ops:
  0.6 36.2 %shard_map.84 = (bf16[256,1024]{1,0:T(8,128)(2,1)S(1)}, bf16[256,1024]{1,0:T(8,128)(2,1)S(1)}, bf16[256,128]{1,0:T(8,128)(2,1)S(1)}, bf16[256,128]{1,0:T(8,128)(2,1)S(1)}) custom-call(bf16[256,1024]{1,0:T(8,128)(2,1)} %q_in.1, bf16[256,128]{1,0:T(8,128)(2,1)} %k_in.1, bf16[256,128]{1,0:T(8,128)(2,1)} %v_in.1, bf16[256,1024]{1,0:T(8,128)(2,1)} %g_in.1, s32[341]{0:T(512)} %doc_in.1), custom_call_target="tpu_custom_call" | custom-call | flops 3221225472 | bytes 2359296 | tf_op jit(solution)/shard_map/pallas_call | solution.py:433
  36.8 1.0 %shard_map.85 = (bf16[256,1024]{1,0:T(8,128)(2,1)}, bf16[256,1024]{1,0:T(8,128)(2,1)}, bf16[256,128]{1,0:T(8,128)(2,1)}, bf16[256,128]{1,0:T(8,128)(2,1)}) custom-call(bf16[256,1024]{1,0:T(8,128)(2,1)S(1)} %get-tuple-element.8.refs_0_, bf16[256,1024]{1,0:T(8,128)(2,1)S(1)} %get-tuple-element.9.refs_1_, bf16[256,128]{1,0:T(8,128)(2,1)S(1)} %get-tuple-element.10.refs_2_, ...), custom_call_target="tpu_custom_call" | custom-call | tf_op jit(solution)/shard_map/pallas_call | solution.py:478

commit v4 on v3

--- a/solution.py
+++ b/solution.py
@@ -27,7 +27,7 @@
     sizes,
     q_in, k_in, v_in, g_in, doc_in,
     att, dq, dk, dv,
-    docs, q, g, qt, gt, kw, vw, kt, vt, bias, probs, dprobs, low, grad_low, row_max, row_sum, row_dot, block_max,
+    docs, q, g, qgt, kw, vw, kt, vt, bias, probs, dprobs, low, grad_low, row_max, row_sum, row_dot, block_max,
     relay_k, relay_v, key_sum, value_sum, send_k, send_v, got_k, got_v,
     local_sem, send_sem, recv_sem,
 ):
@@ -76,7 +76,9 @@
     def greet(place):
         pl.semaphore_signal(barrier, inc=1, device_id=place, device_id_type=MESH)
 
-    greet(sibling)
+    @pl.when(is_odd)
+    def _():
+        greet(sibling)
 
     @pl.when(has_two_before)
     def _():
@@ -170,7 +172,7 @@
 
     key_load.wait()
     value_load.wait()
-    targets = 1 + jnp.where(has_two_after, 1, 0)
+    targets = 1 - odd + jnp.where(has_two_after, 1, 0)
     targets += jnp.where(is_odd & has_three_after, 1, 0)
     targets += jnp.where(is_odd & has_relay_target, 1, 0)
     pl.semaphore_wait(barrier, targets)
@@ -197,8 +199,8 @@
     def _(part):
         for offset in range(UNROLL):
             head = part * UNROLL + offset
-            qt[head] = q[of_head(head)].T
-            gt[head] = g[of_head(head)].T
+            qgt[head, :dim] = q[of_head(head)].T
+            qgt[head, dim:] = g[of_head(head)].T
 
     @pl.when(is_even & has_two_after)
     def _():
@@ -214,10 +216,19 @@
 
     def multiply(slot, part, place):
         head = part * UNROLL + place
-        scores = dot(kw[slot], qt[head]) + bias[slot]
+        nothing = jnp.zeros((tok, dim), BF16)
+        keys_over_values = jnp.concatenate(
+            [
+                jnp.concatenate([kw[slot], nothing], axis=1),
+                jnp.concatenate([nothing, vw[slot]], axis=1),
+            ],
+            axis=0,
+        )
+        both = dot(keys_over_values, qgt[head])
+        scores = both[:tok] + bias[slot]
         probs[place][slot, part] = scores
         top = jnp.max(folded(scores, jnp.max), axis=0, keepdims=True)
-        dprobs[place][slot, part] = dot(vw[slot], gt[head])
+        dprobs[place][slot, part] = both[tok:]
         return jnp.maximum(row_max[place][part], top)
 
     def weigh(slot, part, place, top):
@@ -257,13 +268,17 @@
                     arrived.wait_recv()
                     onward.start()
 
-            @pl.when(is_odd & has_two_before)
+            @pl.when(is_odd)
             def _():
-                for arrived, onward in zip(to_next, passed_to_sibling):
-                    arrived.wait_recv()
-                    onward.start()
-
-            @pl.when(is_odd | has_two_before)
+                received(own_to_sibling)
+
+                @pl.when(has_two_before)
+                def _():
+                    for arrived, onward in zip(to_next, passed_to_sibling):
+                        arrived.wait_recv()
+                        onward.start()
+
+            @pl.when(is_even & has_two_before)
             def _():
                 received(own_to_sibling)
 
@@ -301,13 +316,17 @@
                 if first + GROUP < UNROLL:
                     for place in group:
                         grade(slot, part, place + GROUP)
-                side_by_side = [
-                    jnp.concatenate([ref[place][part, slot] for place in group], axis=1)
-                    for ref in (grad_low, low)
-                ]
+                grads_over_weights = jnp.concatenate(
+                    [
+                        jnp.concatenate([ref[place][part, slot] for place in group], axis=1)
+                        for ref in (grad_low, low)
+                    ],
+                    axis=0,
+                )
                 rows = of_head(part * UNROLL + first, GROUP)
-                keys += dot(side_by_side[0], q[rows])
-                values += dot(side_by_side[1], g[rows])
+                both = dot(grads_over_weights, jnp.concatenate([q[rows], g[rows]], axis=1))
+                keys += both[:tok, :dim]
+                values += both[tok:, dim:]
             key_sum[...] = keys
             value_sum[...] = values
 
@@ -439,8 +458,7 @@
             pltpu.VMEM(doc_starts.shape, jnp.int32),
             pltpu.VMEM((heads * tok, dim), BF16),
             pltpu.VMEM((heads * tok, dim), BF16),
-            pltpu.VMEM((heads, dim, tok), BF16),
-            pltpu.VMEM((heads, dim, tok), BF16),
+            pltpu.VMEM((heads, 2 * dim, tok), BF16),
             pltpu.VMEM((SPAN, tok, dim), BF16),
             pltpu.VMEM((SPAN, tok, dim), BF16),
             pltpu.VMEM((dim, SPAN * tok), BF16),

time: 38 us -> 38.2 us (level)
  the two profiles are of different devices: /device:TPU:5 before, /device:TPU:3 now
where the time goes in v4:
time: 38.2 us; the launch traced here: 38 us
  Pallas kernels  37.3 us (98%)
  between operations  0.64 us (2%)
    pallas_call x1, Pallas kernels, local(): pl.pallas_call(functools.partial(kernel, sizes), out_shape=tuple((pltpu.V...  36.3 us
    pallas_call x1, Pallas kernels, local(): pl.pallas_call(write_out, out_shape=shapes, in_specs=[anywhere] * 4, out_...  1.03 us

profile of v4, /device:TPU:3, one launch (start us, length us, event | category | flops | bytes accessed | tf_op | source)
XLA Modules:
  0.0 38.0 jit_solution(12044989684994368712)
XLA Ops:
  0.6 36.3 %shard_map.84 = (bf16[256,1024]{1,0:T(8,128)(2,1)S(1)}, bf16[256,1024]{1,0:T(8,128)(2,1)S(1)}, bf16[256,128]{1,0:T(8,128)(2,1)S(1)}, bf16[256,128]{1,0:T(8,128)(2,1)S(1)}) custom-call(bf16[256,1024]{1,0:T(8,128)(2,1)} %q_in.1, bf16[256,128]{1,0:T(8,128)(2,1)} %k_in.1, bf16[256,128]{1,0:T(8,128)(2,1)} %v_in.1, bf16[256,1024]{1,0:T(8,128)(2,1)} %g_in.1, s32[341]{0:T(512)} %doc_in.1), custom_call_target="tpu_custom_call" | custom-call | flops 3221225472 | bytes 2359296 | tf_op jit(solution)/shard_map/pallas_call | solution.py:452
  37.0 1.0 %shard_map.85 = (bf16[256,1024]{1,0:T(8,128)(2,1)}, bf16[256,1024]{1,0:T(8,128)(2,1)}, bf16[256,128]{1,0:T(8,128)(2,1)}, bf16[256,128]{1,0:T(8,128)(2,1)}) custom-call(bf16[256,1024]{1,0:T(8,128)(2,1)S(1)} %get-tuple-element.8.refs_0_, bf16[256,1024]{1,0:T(8,128)(2,1)S(1)} %get-tuple-element.9.refs_1_, bf16[256,128]{1,0:T(8,128)(2,1)S(1)} %get-tuple-element.10.refs_2_, ...), custom_call_target="tpu_custom_call" | custom-call | tf_op jit(solution)/shard_map/pallas_call | solution.py:496

commit v5 on v3

--- a/solution.py
+++ b/solution.py
@@ -76,7 +76,9 @@
     def greet(place):
         pl.semaphore_signal(barrier, inc=1, device_id=place, device_id_type=MESH)
 
-    greet(sibling)
+    @pl.when(is_odd)
+    def _():
+        greet(sibling)
 
     @pl.when(has_two_before)
     def _():
@@ -170,7 +172,7 @@
 
     key_load.wait()
     value_load.wait()
-    targets = 1 + jnp.where(has_two_after, 1, 0)
+    targets = 1 - odd + jnp.where(has_two_after, 1, 0)
     targets += jnp.where(is_odd & has_three_after, 1, 0)
     targets += jnp.where(is_odd & has_relay_target, 1, 0)
     pl.semaphore_wait(barrier, targets)
@@ -257,13 +259,17 @@
                     arrived.wait_recv()
                     onward.start()
 
-            @pl.when(is_odd & has_two_before)
+            @pl.when(is_odd)
             def _():
-                for arrived, onward in zip(to_next, passed_to_sibling):
-                    arrived.wait_recv()
-                    onward.start()
-
-            @pl.when(is_odd | has_two_before)
+                received(own_to_sibling)
+
+                @pl.when(has_two_before)
+                def _():
+                    for arrived, onward in zip(to_next, passed_to_sibling):
+                        arrived.wait_recv()
+                        onward.start()
+
+            @pl.when(is_even & has_two_before)
             def _():
                 received(own_to_sibling)
 
@@ -286,8 +292,7 @@
 
     @pl.loop(0, SPAN)
     def _(turn):
-        even_slot = jnp.where(turn == 0, 1, jnp.where(turn == 1, 3, 2))
-        slot = jnp.where(turn == 3, 0, jnp.where(is_odd, 3 - turn, even_slot))
+        slot = jnp.where(turn == 3, 0, jnp.where(is_odd, 3 - turn, 1 + turn))
         key_sum[...] = jnp.zeros_like(key_sum)
         value_sum[...] = jnp.zeros_like(value_sum)
 
@@ -348,8 +353,8 @@
             columns = pl.ds(pl.multiple_of((part * UNROLL + place) * dim, dim), dim)
             weights = low[place][part].reshape(SPAN * tok, tok)
             grads = grad_low[place][part].reshape(SPAN * tok, tok)
-            att[:, columns] = dot(vt[...], weights).T.astype(BF16)
-            dq[:, columns] = (dot(kt[...], grads) * score_scale).T.astype(BF16)
+            att[:, columns] = dot(vt[...], weights).astype(BF16).T
+            dq[:, columns] = (dot(kt[...], grads) * score_scale).astype(BF16).T
 
     @pl.when(is_even)
     def _():

time: 38 us -> 39.1 us (1.029)
  the two profiles are of different devices: /device:TPU:5 before, /device:TPU:61 now
where the time goes in v5:
time: 39.1 us; the launch traced here: 38.9 us
  Pallas kernels  38.2 us (98%)
  between operations  0.64 us (2%)
    pallas_call x1, Pallas kernels, local(): pl.pallas_call(functools.partial(kernel, sizes), out_shape=tuple((pltpu.V...  37.2 us
    pallas_call x1, Pallas kernels, local(): pl.pallas_call(write_out, out_shape=shapes, in_specs=[anywhere] * 4, out_...  1.03 us

profile of v5, /device:TPU:61, one launch (start us, length us, event | category | flops | bytes accessed | tf_op | source)
XLA Modules:
  0.0 38.9 jit_solution(10183610208275454931)
XLA Ops:
  0.6 37.2 %shard_map.84 = (bf16[256,1024]{1,0:T(8,128)(2,1)S(1)}, bf16[256,1024]{1,0:T(8,128)(2,1)S(1)}, bf16[256,128]{1,0:T(8,128)(2,1)S(1)}, bf16[256,128]{1,0:T(8,128)(2,1)S(1)}) custom-call(bf16[256,1024]{1,0:T(8,128)(2,1)} %q_in.1, bf16[256,128]{1,0:T(8,128)(2,1)} %k_in.1, bf16[256,128]{1,0:T(8,128)(2,1)} %v_in.1, bf16[256,1024]{1,0:T(8,128)(2,1)} %g_in.1, s32[341]{0:T(512)} %doc_in.1), custom_call_target="tpu_custom_call" | custom-call | flops 3221225472 | bytes 2359296 | tf_op jit(solution)/shard_map/pallas_call | solution.py:438
  37.9 1.0 %shard_map.85 = (bf16[256,1024]{1,0:T(8,128)(2,1)}, bf16[256,1024]{1,0:T(8,128)(2,1)}, bf16[256,128]{1,0:T(8,128)(2,1)}, bf16[256,128]{1,0:T(8,128)(2,1)}) custom-call(bf16[256,1024]{1,0:T(8,128)(2,1)S(1)} %get-tuple-element.8.refs_0_, bf16[256,1024]{1,0:T(8,128)(2,1)S(1)} %get-tuple-element.9.refs_1_, bf16[256,128]{1,0:T(8,128)(2,1)S(1)} %get-tuple-element.10.refs_2_, ...), custom_call_target="tpu_custom_call" | custom-call | tf_op jit(solution)/shard_map/pallas_call | solution.py:483

commit v6 on v1

--- a/solution.py
+++ b/solution.py
@@ -25,10 +25,10 @@
 def kernel(
     sizes,
     q_in, k_in, v_in, g_in, doc_in,
-    att_out, dq_out, dk_out, dv_out,
+    att, dq, dk, dv,
     docs, q, g, qt, gt, kw, vw, kt, vt, bias, probs, dprobs, low, grad_low, row_max, row_sum, row_dot, block_max,
-    relay_k, relay_v, part_k, part_v, send_k, send_v, got_k, got_v, att, dq, dk, dv,
-    local_sem, out_sem, send_sem, recv_sem,
+    relay_k, relay_v, part_k, part_v, send_k, send_v, got_k, got_v,
+    local_sem, send_sem, recv_sem,
 ):
     outer_count, inner_count, tok, heads, dim = sizes
     total = outer_count * inner_count
@@ -152,25 +152,6 @@
         for copy in copies:
             copy.wait_send()
 
-    key_load.wait()
-    value_load.wait()
-    targets = 1 + jnp.where(has_two_after, 1, 0)
-    targets += jnp.where(is_odd & has_three_after, 1, 0)
-    targets += jnp.where(is_odd & has_relay_target, 1, 0)
-    pl.semaphore_wait(barrier, targets)
-
-    @pl.when(is_even)
-    def _():
-        start(own_to_sibling)
-
-    @pl.when(is_odd & has_two_after)
-    def _():
-        start(to_next)
-
-    @pl.when(is_odd & has_three_after)
-    def _():
-        start(relay_in)
-
     doc_load.wait()
     first_row = (me * tok).astype(F32)
     doc_starts = jnp.broadcast_to(docs[...][None, :].astype(F32), (tok, docs.shape[0])) - first_row
@@ -185,6 +166,25 @@
         if age == 0:
             allowed = allowed & (places <= lax.broadcasted_iota(jnp.int32, (tok, tok), 1))
         bias[age] = jnp.where(allowed, 0.0, MASKED)
+
+    key_load.wait()
+    value_load.wait()
+    targets = 1 + jnp.where(has_two_after, 1, 0)
+    targets += jnp.where(is_odd & has_three_after, 1, 0)
+    targets += jnp.where(is_odd & has_relay_target, 1, 0)
+    pl.semaphore_wait(barrier, targets)
+
+    @pl.when(is_even)
+    def _():
+        start(own_to_sibling)
+
+    @pl.when(is_odd & has_two_after)
+    def _():
+        start(to_next)
+
+    @pl.when(is_odd & has_three_after)
+    def _():
+        start(relay_in)
 
     def of_head(head, count=1):
         return slice(head * tok, (head + count) * tok)
@@ -341,13 +341,8 @@
         turn(slot)
     for head in range(heads):
         columns = slice(head * dim, (head + 1) * dim)
-        att[:, columns] = dot(vt[...], low[head]).T.astype(BF16)
-        dq[:, columns] = (dot(kt[...], grad_low[head]) * score_scale).T.astype(BF16)
-    att_copy = pltpu.make_async_copy(att, att_out, out_sem.at[0])
-    att_copy.start()
-    dq_copy = pltpu.make_async_copy(dq, dq_out, out_sem.at[1])
-    dq_copy.start()
-
+        att[:, columns] = dot(vt[...], low[head]).astype(BF16).T
+        dq[:, columns] = (dot(kt[...], grad_low[head]) * score_scale).astype(BF16).T
     @pl.when(is_even)
     def _():
         received(first)
@@ -364,11 +359,7 @@
         received(second)
 
     dk[...] = ((part_k[0] + got_k[2].astype(F32)) * score_scale).astype(BF16)
-    dk_copy = pltpu.make_async_copy(dk, dk_out, out_sem.at[2])
-    dk_copy.start()
     dv[...] = (part_v[0] + got_v[2].astype(F32)).astype(BF16)
-    dv_copy = pltpu.make_async_copy(dv, dv_out, out_sem.at[3])
-    dv_copy.start()
 
     @pl.when(has_two_after)
     def _():
@@ -401,9 +392,6 @@
     @pl.when(has_two_before)
     def _():
         sent(second)
-
-    for copy in (att_copy, dq_copy, dk_copy, dv_copy):
-        copy.wait()
 
 
 def write_out(*refs):
@@ -437,7 +425,7 @@
         functools.partial(kernel, sizes),
         out_shape=tuple(pltpu.VMEM(shape.shape, shape.dtype) for shape in shapes),
         in_specs=[pl.BlockSpec(memory_space=pltpu.HBM)] * 5,
-        out_specs=(anywhere,) * 4,
+        out_specs=(pl.BlockSpec(memory_space=pltpu.VMEM),) * 4,
         scratch_shapes=[
             pltpu.VMEM(doc_starts.shape, jnp.int32),
             pltpu.VMEM((heads * tok, dim), BF16),
@@ -465,12 +453,7 @@
             pltpu.VMEM((SPAN - 1, tok, dim), BF16),
             pltpu.VMEM((SPAN - 1, tok, dim), BF16),
             pltpu.VMEM((SPAN - 1, tok, dim), BF16),
-            pltpu.VMEM((tok, width), BF16),
-            pltpu.VMEM((tok, width), BF16),
-            pltpu.VMEM((tok, dim), BF16),
-            pltpu.VMEM((tok, dim), BF16),
             pltpu.SemaphoreType.DMA((3 + 2 * heads,)),
-            pltpu.SemaphoreType.DMA((4,)),
             pltpu.SemaphoreType.DMA((14,)),
             pltpu.SemaphoreType.DMA((14,)),
         ],

time: 37.7 us -> 37.6 us (level)
  no operation moved by 1% of the time
where the time goes in v6:
time: 37.6 us; the launch traced here: 37.3 us
  Pallas kernels  36.7 us (98%)
  between operations  0.64 us (2%)
    pallas_call x1, Pallas kernels, local(): pl.pallas_call(functools.partial(kernel, sizes), out_shape=tuple((pltpu.V...  35.7 us
    pallas_call x1, Pallas kernels, local(): pl.pallas_call(write_out, out_shape=shapes, in_specs=[anywhere] * 4, out_...  1.03 us

profile of v6, /device:TPU:28, one launch (start us, length us, event | category | flops | bytes accessed | tf_op | source)
XLA Modules:
  0.0 37.3 jit_solution(4884439803742789833)
XLA Ops:
  0.6 35.7 %shard_map.84 = (bf16[256,1024]{1,0:T(8,128)(2,1)S(1)}, bf16[256,1024]{1,0:T(8,128)(2,1)S(1)}, bf16[256,128]{1,0:T(8,128)(2,1)S(1)}, bf16[256,128]{1,0:T(8,128)(2,1)S(1)}) custom-call(bf16[256,1024]{1,0:T(8,128)(2,1)} %q_in.1, bf16[256,128]{1,0:T(8,128)(2,1)} %k_in.1, bf16[256,128]{1,0:T(8,128)(2,1)} %v_in.1, bf16[256,1024]{1,0:T(8,128)(2,1)} %g_in.1, s32[341]{0:T(512)} %doc_in.1), custom_call_target="tpu_custom_call" | custom-call | flops 3221225472 | bytes 2359296 | tf_op jit(solution)/shard_map/pallas_call | solution.py:424
  36.3 1.0 %shard_map.85 = (bf16[256,1024]{1,0:T(8,128)(2,1)}, bf16[256,1024]{1,0:T(8,128)(2,1)}, bf16[256,128]{1,0:T(8,128)(2,1)}, bf16[256,128]{1,0:T(8,128)(2,1)}) custom-call(bf16[256,1024]{1,0:T(8,128)(2,1)S(1)} %get-tuple-element.8.refs_0_, bf16[256,1024]{1,0:T(8,128)(2,1)S(1)} %get-tuple-element.9.refs_1_, bf16[256,128]{1,0:T(8,128)(2,1)S(1)} %get-tuple-element.10.refs_2_, ...), custom_call_target="tpu_custom_call" | custom-call | tf_op jit(solution)/shard_map/pallas_call | solution.py:469
